TPU v7x, 512 devices: a whole 4x8x8 slice. The times are simulated.
512 devices in a mesh: row: 16 (over x, y_hi, core), col: 32 (over y_lo, z).
Axes of the slice: x: 4, y: 8 (y_hi: 2, y_lo: 4; y = y_hi * 4 + y_lo), z: 8, core: 2. Of those that a mesh axis runs over, the one named last changes fastest.
Arguments:
- points: bfloat16 [16384, 256], P(('row', 'col')), may hold values from -6 to 6
- basis: float32 [16384, 64], P(('row', 'col')), may hold values from -6 to 6
Outputs:
- basis_out: float32 [16384, 64], P(('row', 'col'))
- degree: float32 [16384], P(('row', 'col'))
All inputs are finite; a program needn't handle non-finite values.
Results may differ from a plain program's by a relative error of at most 0.0003.
Values may be sent and summed in bfloat16 or wider, within the bound.
No kernel may reach another device: no remote copies, remote signals or barrier semaphores. Data moves between devices by JAX's collectives and lax.ppermute only.
A program may use at most 64 MiB of HBM per device.

v0:
```python
import jax
import jax.numpy as jnp
from jax import lax
from jax.sharding import PartitionSpec as P

ITERS = 2


def affinity(rows_blk, rows_sq, cols_pts, cols_sq, width):
    dots = lax.dot_general(
        rows_blk, cols_pts, (((1,), (1,)), ((), ())), preferred_element_type=jnp.float32
    )
    dist = rows_sq[:, None] + cols_sq[None, :] - 2.0 * dots
    return jnp.exp(-dist / (0.25 * width))


def sum_squares(values):
    floats = values.astype(jnp.float32)
    return jnp.sum(floats * floats, axis=1)


def per_device(points, basis):
    width = points.shape[1]
    row_pts = lax.all_gather(points, "col", axis=0, tiled=True)
    col_pts = lax.all_gather(points, "row", axis=0, tiled=True)
    row_sq = sum_squares(row_pts)
    col_sq = sum_squares(col_pts)
    nrows = row_pts.shape[0]
    ncols = col_pts.shape[0]
    block = min(512, nrows)
    nblocks = nrows // block
    row_blocks = row_pts.reshape(nblocks, block, width)
    sq_blocks = row_sq.reshape(nblocks, block)
    order = jnp.arange(nblocks, dtype=jnp.int32)

    def tile(index):
        return affinity(row_blocks[index], sq_blocks[index], col_pts, col_sq, width)

    def first_pass(carry, index):
        weights = tile(index)
        outputs = (jnp.sum(weights, axis=1),)
        return (carry + jnp.sum(weights, axis=0), outputs)

    col_sums, outputs = lax.scan(first_pass, jnp.zeros((ncols,), jnp.float32), order)
    row_sums = outputs[0].reshape(nrows)

    def tile_full(index):
        return tile(index)

    degree = lax.psum_scatter(row_sums, "col", scatter_dimension=0, tiled=True)
    inv_root = lax.rsqrt(degree)
    for step in range(ITERS):
        scaled = basis * inv_root[:, None]
        col_basis = lax.all_gather(scaled, "row", axis=0, tiled=True)
        partial_rows = lax.map(
            lambda index: jnp.dot(tile_full(index), col_basis, precision=lax.Precision.HIGHEST),
            order,
        )
        product = lax.psum_scatter(
            partial_rows.reshape(nrows, -1), "col", scatter_dimension=0, tiled=True
        )
        update = product * inv_root[:, None]
        gram = lax.psum(jnp.dot(update.T, update, precision=lax.Precision.HIGHEST), ("row", "col"))
        factor = jnp.linalg.cholesky(gram)
        basis = jax.scipy.linalg.solve_triangular(factor, update.T, lower=True).T
    return (basis, degree)


def solution(mesh):
    return jax.shard_map(
        per_device,
        mesh=mesh,
        in_specs=(P(("row", "col"), None), P(("row", "col"), None)),
        out_specs=(P(("row", "col"), None), P(("row", "col"))),
        check_vma=False,
    )
```

profile of v0, /device:TPU:1, one launch (start us, length us, event | category | flops | bytes accessed | tf_op | source)
XLA Modules:
  0.0 816.4 jit_solution(5303512780511332264)
XLA Ops:
  7.2 34.5 %all_gather.13 = bf16[512,256]{1,0:T(8,128)(2,1)S(1)} all-gather(bf16[32,256]{1,0:T(8,128)(2,1)} %param.11), channel_id=1, replica_groups=mesh['row'=16,'col'=32] {'row'}, dimensions={0}, use_global_device_ids=true | all-gather | bytes 278528 | tf_op jit(solution)/shard_map/all_gather | solution.py:25
  41.7 71.0 %all_gather.12 = bf16[1024,256]{1,0:T(8,128)(2,1)S(1)} all-gather(bf16[32,256]{1,0:T(8,128)(2,1)S(1)} %copy-done), channel_id=1, replica_groups=mesh['row'=16,'col'=32] {'col'}, dimensions={0}, use_global_device_ids=true | all-gather | bytes 540672 | tf_op jit(solution)/shard_map/all_gather | solution.py:24
  113.1 6.5 while.30
  113.1 0.7 dynamic_slice.54
  116.4 0.7 dynamic_slice.54
  119.7 60.7 %all-reduce = f32[1024]{0:T(1024)S(1)} all-reduce(f32[1024]{0:T(1024)S(1)} %bitcast.112), channel_id=2, replica_groups=mesh['row'=16,'col'=32] {'col'}, use_global_device_ids=true, to_apply=%region_5.6.clone | all-reduce | flops 1024 | bytes 8192
  180.4 1.3 dynamic-slice
  182.9 53.3 %all_gather.14 = f32[512,64]{1,0:T(8,128)S(1)} all-gather(f32[32,64]{1,0:T(8,128)S(1)} %broadcast_multiply_fusion), channel_id=1, replica_groups=mesh['row'=16,'col'=32] {'row'}, dimensions={0}, use_global_device_ids=true | all-gather | bytes 139264 | tf_op jit(solution)/shard_map/all_gather | solution.py:54
  236.3 8.7 %while.31 = (s32[]{:T(128)}, f32[2,512,64]{1,2,0:T(8,128)S(1)}, s32[2]{0:T(128)S(1)}, f32[2,512]{1,0:T(2,128)S(1)}, f32[512]{0:T(512)S(1)}, /*index=5*/bf16[2,51...) while((s32[]{:T(128)}, f32[2,512,64]{1,2,0:T(8,128)S(1)}, ...), condition=%wide.region_7.8_spmd, body=%wide.region_6.7_spmd.sunk | while | flops 336855040 | bytes 3023015 | solution.py:55
  236.3 0.7 dynamic_slice.57
  239.5 1.2 fusion.76
  243.8 1.2 fusion.76
  245.0 1.0 copy.30
  246.0 130.7 %reduce-scatter.7.cloned.1.call-done = f32[32,64]{1,0:T(8,128)} async-done(((f32[1024,64]{1,0:T(8,128)}), f32[32,64]{1,0:T(8,128)}) %reduce-scatter.7.cloned.1.call-update) | async-done | bytes 8208 | tf_op jit(solution)/shard_map/reduce_scatter | solution.py:59
  376.7 1.1 fusion.39
  377.8 118.8 %psum.14 = f32[64,64]{0,1:T(8,128)S(1)} all-reduce(f32[64,64]{0,1:T(8,128)S(1)} %fusion.39), channel_id=1, replica_groups=mesh['row'=16,'col'=32] {'row','col'}, use_global_device_ids=true, to_apply=%region_9.10 | all-reduce | flops 4096 | bytes 32768 | tf_op jit(solution)/shard_map/psum | solution.py:63
  496.7 5.8 cholesky.44
  502.6 0.7 compare_reduce_fusion.1
  503.3 0.7 fusion.25
  504.1 4.9 custom-call.6
  509.2 28.9 %all_gather.15 = f32[512,64]{1,0:T(8,128)S(1)} all-gather(f32[32,64]{1,0:T(8,128)S(1)} %fusion.24), channel_id=1, replica_groups=mesh['row'=16,'col'=32] {'row'}, dimensions={0}, use_global_device_ids=true | all-gather | bytes 139264 | tf_op jit(solution)/shard_map/all_gather | solution.py:54
  538.1 8.7 %while.32 = (s32[]{:T(128)}, f32[2,512,64]{1,2,0:T(8,128)S(1)}, s32[2]{0:T(128)S(1)}, f32[2,512]{1,0:T(2,128)S(1)}, f32[512]{0:T(512)S(1)}, /*index=5*/bf16[2,51...) while((s32[]{:T(128)}, f32[2,512,64]{1,2,0:T(8,128)S(1)}, ...), condition=%wide.region_13.16_spmd, body=%wide.region_12.15_spmd.sunk | while | flops 336855040 | bytes 3023015 | solution.py:55
  541.3 1.2 fusion.82
  542.5 0.7 dynamic_slice.60
  545.6 1.2 fusion.82
  546.8 1.0 copy.31
  547.8 128.5 %reduce-scatter.9.cloned.1.call-done = f32[32,64]{1,0:T(8,128)} async-done(((f32[1024,64]{1,0:T(8,128)}), f32[32,64]{1,0:T(8,128)}) %reduce-scatter.9.cloned.1.call-update) | async-done | bytes 8208 | tf_op jit(solution)/shard_map/reduce_scatter | solution.py:59
  676.4 1.1 fusion.36
  677.5 119.0 %psum.15 = f32[64,64]{0,1:T(8,128)S(1)} all-reduce(f32[64,64]{0,1:T(8,128)S(1)} %fusion.36), channel_id=1, replica_groups=mesh['row'=16,'col'=32] {'row','col'}, use_global_device_ids=true, to_apply=%region_15.18 | all-reduce | flops 4096 | bytes 32768 | tf_op jit(solution)/shard_map/psum | solution.py:63
  796.6 5.8 cholesky.55
  803.8 4.9 custom-call.7
  808.7 0.8 convolution_bitcast_fusion.2
  (49 shorter events, 6.9 us)
Async XLA Ops:
  7.2 34.5 %copy-start = (bf16[32,256]{1,0:T(8,128)(2,1)S(1)}, bf16[32,256]{1,0:T(8,128)(2,1)}, u32[]{:S(2)}) copy-start(bf16[32,256]{1,0:T(8,128)(2,1)} %param.11) | copy-start | bytes 49156
  7.2 369.6 %reduce-scatter.7.cloned.1.call-start = ((), (), s32[]{:S(2)}) async-start(), calls=%async_computation.2 | async-start | bytes 540672 | tf_op jit(solution)/shard_map/reduce_scatter | solution.py:59
  119.7 63.2 %copy-start.1 = (f32[32,64]{1,0:T(8,128)S(1)}, f32[32,64]{1,0:T(8,128)}, u32[]{:S(2)}) copy-start(f32[32,64]{1,0:T(8,128)} %param.12) | copy-start | bytes 24580
  246.0 430.4 %reduce-scatter.9.cloned.1.call-start = ((), (), s32[]{:S(2)}) async-start(), calls=%async_computation.3 | async-start | bytes 540672 | tf_op jit(solution)/shard_map/reduce_scatter | solution.py:59
  503.3 5.6 copy-start.2
  803.1 5.6 copy-start.3
Sparse Core Ops, SparseCore 0:
  246.1 130.5 reduce-scatter.6
  547.9 128.3 reduce-scatter.8
where the time goes:
time: 817 us; the launch traced here: 816 us
  blocking collectives  486 us (59%)
  waiting for transfers between devices  259 us (32%)
  other arithmetic  24.7 us (3%)
  between operations  14.9 us (2%)
  loops' own time  12.6 us (2%)
  matrix products  10.4 us (1%)
  local copies, waits for them, and re-layouts  8.22 us (1%)
    reduce_scatter x2, waiting for transfers between devices, per_device(): lax.psum_scatter(partial_rows.reshape(nrows, -1), 'col', scatter_dimensio...  259 us
    psum x2, blocking collectives, per_device(): lax.psum(jnp.dot(update.T, update, precision=lax.Precision.HIGHEST), ('ro...  238 us
    all_gather x2, blocking collectives, per_device(): col_basis = lax.all_gather(scaled, 'row', axis=0, tiled=True)  82.2 us
    all_gather x1, blocking collectives, per_device(): row_pts = lax.all_gather(points, 'col', axis=0, tiled=True)  71 us
    unnamed x1, blocking collectives  60.7 us
    all_gather x1, blocking collectives, per_device(): col_pts = lax.all_gather(points, 'row', axis=0, tiled=True)  34.5 us
  transfers between devices with their start and end apart: 2, of which 2 were waited for; matrix products, arithmetic and copies ran while one was open for 0% of the time, Pallas kernels for 0%

commit v1 on v0

v1 whole, which is shorter than its diff:
```python
import functools
import math

import jax
import jax.numpy as jnp
from jax import lax
from jax.experimental import pallas as pl
from jax.experimental.pallas import tpu as pltpu
from jax.sharding import Mesh, PartitionSpec as P

AXES = ("x", "yh", "core", "yl", "z")
SIZES = (4, 2, 2, 4, 8)
A_AXES = ("core", "yh", "yl")
B_AXES = ("x", "z")
NA, NB = 16, 32
HIGH = lax.Precision.HIGHEST
F32 = jnp.float32
VMEM = pl.BlockSpec(memory_space=pltpu.VMEM)
SMEM = pl.BlockSpec(memory_space=pltpu.SMEM)


def exchange(chunks, axes):
    return lax.all_to_all(chunks, axes, 0, 0, tiled=True)


def call(body, outs, *args, specs=None, scratch=(), name=None):
    return pl.pallas_call(
        body,
        out_shape=outs,
        in_specs=specs or [VMEM] * len(args),
        out_specs=[VMEM] * len(outs),
        scratch_shapes=list(scratch),
        compiler_params=pltpu.CompilerParams(vmem_limit_bytes=48 * 1024 * 1024),
        name=name,
    )(*args)


def fold(block):
    half = block.shape[0] // 2
    return jnp.concatenate([block[:half], block[half:]], axis=1)


def unfold(packed):
    return jnp.concatenate([packed[:, :64], packed[:, 64:]], axis=0)


def inverse_cholesky(gram):
    n = gram.shape[0]
    tiles = []
    sub = lax.broadcasted_iota(jnp.int32, (8, 128), 0)
    lane = lax.broadcasted_iota(jnp.int32, (8, 128), 1)
    for t in range(n // 8):
        eye = jnp.where(lane == sub + 8 * t + n, 1.0, 0.0).astype(F32)
        left = jnp.concatenate([gram[8 * t : 8 * t + 8], jnp.zeros((8, n), F32)], axis=1)
        tiles.append(left + eye)
    scale = [jnp.ones((8, 128), F32) for _ in tiles]
    group = 4
    for k in range(0, n, group):
        top = k // 8
        cols = [
            {t: jnp.broadcast_to(tiles[t][:, k + j : k + j + 1], (8, 128)) for t in range(top, n // 8)}
            for j in range(group)
        ]
        for j in range(group):
            r = (k + j) % 8
            pivot = jnp.broadcast_to(cols[j][top][r : r + 1], (8, 128))
            scale[top] = jnp.where(sub == r, lax.rsqrt(pivot), scale[top])
            inv = 1.0 / pivot
            row = jnp.broadcast_to(tiles[top][r : r + 1], (8, 128))
            heads = [jnp.broadcast_to(cols[i][top][r : r + 1], (8, 128)) for i in range(j + 1, group)]
            for t in range(top, n // 8):
                factor = cols[j][t] * inv
                if t == top:
                    factor = jnp.where(sub > r, factor, 0.0)
                tiles[t] = tiles[t] - factor * row
                for i in range(j + 1, group):
                    cols[i][t] = cols[i][t] - factor * heads[i - j - 1]
    out = jnp.concatenate([tile * s for tile, s in zip(tiles, scale)], axis=0)
    return out[:, n:]


def weights_kernel(rows_ref, cols_ref, basis_ref, w_ref, out_ref):
    rows, cols = rows_ref[...], cols_ref[...]
    width = rows.shape[1]
    dots = lax.dot_general(rows, cols, (((1,), (1,)), ((), ())), preferred_element_type=F32)
    rows32, cols32 = rows.astype(F32), cols.astype(F32)
    rows_sq = jnp.sum(rows32 * rows32, axis=1, keepdims=True)
    cols_sq = jnp.sum(cols32 * cols32, axis=1, keepdims=True)
    cols_sq = jnp.transpose(jnp.broadcast_to(cols_sq, (cols_sq.shape[0], 128)))[:1]
    dist = rows_sq + cols_sq - 2.0 * dots
    weights = jnp.exp(-dist / (0.25 * width))
    w_ref[...] = weights
    sums = jnp.sum(weights, axis=0, keepdims=True)
    head = jnp.concatenate([sums[:, 128 * i : 128 * i + 128] for i in range(4)] + [jnp.zeros((4, 128), F32)], axis=0)
    payload = jnp.concatenate([head, fold(basis_ref[...])], axis=0)
    for i in range(NA):
        out_ref[i] = payload


def first_kernel(me_ref, w_ref, in_ref, part_ref, dinv_ref, deg_ref, column_ref):
    head = in_ref[0, :8]
    for i in range(1, NA):
        head = head + in_ref[i, :8]
    mine = me_ref[0]
    picked = jnp.where(lax.broadcasted_iota(jnp.int32, (8, 128), 0) == mine // 4, head, 0.0)
    picked = jnp.broadcast_to(jnp.sum(picked, axis=0, keepdims=True), (8, 128))
    deg_ref[...] = pltpu.roll(picked, (128 - 32 * (mine % 4)) % 128, 1)
    turned = jnp.transpose(lax.rsqrt(head))
    column = jnp.concatenate([turned[:, i : i + 1] for i in range(4)], axis=0)
    column_ref[...] = jnp.broadcast_to(column, column_ref.shape)
    dinv_ref[...] = fold(column_ref[pl.ds(pl.multiple_of(mine * 32, 32), 32)][:, :64])
    scaled = jnp.concatenate([unfold(in_ref[i, 8:]) for i in range(NA)], axis=0) * column
    part = jnp.dot(w_ref[...], scaled, precision=HIGH, preferred_element_type=F32)
    for i in range(NB):
        part_ref[i] = fold(part[32 * i : 32 * i + 32])


def update_kernel(in_ref, dinv_ref, out_ref):
    total = in_ref[0]
    for i in range(1, NB):
        total = total + in_ref[i]
    dinv = dinv_ref[...]
    update = total * dinv
    lane = lax.broadcasted_iota(jnp.int32, (8, 128), 1)
    rider = jnp.where(lane % 64 < 32, dinv[:8], dinv[8:])
    payload = jnp.concatenate([update, rider], axis=0)
    for i in range(NB):
        out_ref[i] = payload


def second_kernel(w_ref, in_ref, out_ref):
    lane = lax.broadcasted_iota(jnp.int32, (8, 128), 1)
    low = lane % 64 < 32
    updates, scaled = [], []
    for i in range(NB):
        update, rider = in_ref[i, :16], in_ref[i, 16:]
        top = jnp.where(low, rider, pltpu.roll(rider, 32, 1))
        bottom = jnp.where(low, pltpu.roll(rider, 96, 1), rider)
        updates.append(update)
        scaled.append(unfold(update * jnp.concatenate([top, bottom], axis=0)))
    packed = jnp.concatenate(updates, axis=0)
    scaled = jnp.concatenate(scaled, axis=0)
    both = lax.dot_general(packed, packed, (((0,), (0,)), ((), ())), precision=HIGH, preferred_element_type=F32)
    gram = fold(both[:64, :64] + both[64:, 64:])
    part = lax.dot_general(w_ref[...], scaled, (((0,), (0,)), ((), ())), precision=HIGH, preferred_element_type=F32)
    for i in range(NA):
        out_ref[i, :16] = fold(part[32 * i : 32 * i + 32])
        out_ref[i, 16:] = gram


def normalize_kernel(in_ref, dinv_ref, update_ref, out_ref):
    total = in_ref[0]
    for i in range(1, NA):
        total = total + in_ref[i]
    update = unfold(total[:16] * dinv_ref[...])
    inverse = inverse_cholesky(unfold(total[16:]))
    update = lax.dot_general(update, inverse, (((1,), (1,)), ((), ())), precision=HIGH, preferred_element_type=F32)
    update_ref[...] = update
    gram = fold(lax.dot_general(update, update, (((0,), (0,)), ((), ())), precision=HIGH, preferred_element_type=F32))
    for i in range(NB):
        out_ref[i] = gram


def relay_kernel(in_ref, out_ref):
    total = in_ref[0]
    for i in range(1, NB):
        total = total + in_ref[i]
    for i in range(NA):
        out_ref[i] = total


def final_kernel(in_ref, update_ref, out_ref):
    total = in_ref[0]
    for i in range(1, NA):
        total = total + in_ref[i]
    inverse = inverse_cholesky(unfold(total))
    out_ref[...] = lax.dot_general(
        update_ref[...], inverse, (((1,), (1,)), ((), ())), precision=HIGH, preferred_element_type=F32
    )


def per_device(points, basis):
    own, width = points.shape
    shape = lambda *dims: jax.ShapeDtypeStruct(dims, F32)
    me = lax.axis_index(A_AXES).astype(jnp.int32).reshape(1)
    row_pts = exchange(jnp.broadcast_to(points[None], (NB, own, width)), B_AXES).reshape(NB * own, width)
    col_pts = exchange(jnp.broadcast_to(points[None], (NA, own, width)), A_AXES).reshape(NA * own, width)
    weights, sums = call(
        weights_kernel, [shape(NB * own, NA * own), shape(NA, 24, 128)], row_pts, col_pts, basis, name="weights"
    )
    sums = exchange(sums, A_AXES)
    part, dinv, degree = call(
        first_kernel,
        [shape(NB, 16, 128), shape(16, 128), shape(8, 128)],
        me,
        weights,
        sums,
        specs=[SMEM, VMEM, VMEM],
        scratch=[pltpu.VMEM((NA * own, 128), F32)],
        name="first_product",
    )
    part = exchange(part, B_AXES)
    (update,) = call(update_kernel, [shape(NB, 24, 128)], part, dinv, name="first_update")
    update = exchange(update, B_AXES)
    (part,) = call(second_kernel, [shape(NA, 48, 128)], weights, update, name="second_product")
    part = exchange(part, A_AXES)
    update, gram = call(normalize_kernel, [shape(own, 64), shape(NB, 32, 128)], part, dinv, name="normalize")
    gram = exchange(gram, B_AXES)
    (gram,) = call(relay_kernel, [shape(NA, 32, 128)], gram, name="relay")
    gram = exchange(gram, A_AXES)
    (out,) = call(final_kernel, [shape(own, 64)], gram, update, name="orthonormalize")
    return (out, degree[0, :own])


def solution(mesh):
    fine = Mesh(mesh.devices.reshape(SIZES), AXES)
    spec = P(AXES)
    return jax.shard_map(
        per_device,
        mesh=fine,
        in_specs=(P(AXES, None), P(AXES, None)),
        out_specs=(P(AXES, None), spec),
        check_vma=False,
    )
```

time: 817 us -> 169 us (0.21)
  blocking collectives: 486 us -> 117 us
  waiting for transfers between devices: 259 us -> 17.2 us
  other arithmetic: 24.7 us -> 0 us
  starting transfers between devices: 0.08 us -> 16.8 us
  between operations: 14.9 us -> 0.67 us
  Pallas kernels: 0 us -> 14 us
  loops' own time: 12.6 us -> 0 us
  matrix products: 10.4 us -> 0 us
    reduce_scatter x2 -> x0, waiting for transfers between devices: 259 us -> none  [per_device(): lax.psum_scatter(partial_rows.reshape(nrows, -1), 'col', scatter_dimensio...]
    psum x2 -> x0, blocking collectives: 238 us -> none  [per_device(): lax.psum(jnp.dot(update.T, update, precision=lax.Precision.HIGHEST), ('ro...]
    all_gather x4 -> x0, blocking collectives: 188 us -> none  [the longest x2 82.2 us: per_device(): col_basis = lax.all_gather(scaled, 'row', axis=0, tiled=True)]
    all_to_all x0 -> x6, blocking collectives: none -> 117 us  [exchange(): return lax.all_to_all(chunks, axes, 0, 0, tiled=True)]
    unnamed x1 -> x0, blocking collectives: 60.7 us -> none
    another operation x10 -> x0, other arithmetic: 24.3 us -> none  [the longest x6 13.1 us: per_device(): factor = jnp.linalg.cholesky(gram)]
    all_to_all x0 -> x2, waiting for transfers between devices: none -> 17.2 us  [exchange(): return lax.all_to_all(chunks, axes, 0, 0, tiled=True)]
    all_to_all x0 -> x2, starting transfers between devices: none -> 16.8 us  [exchange(): return lax.all_to_all(chunks, axes, 0, 0, tiled=True)]
where the time goes in v1:
time: 169 us; the launch traced here: 167 us
  blocking collectives  117 us (69%)
  waiting for transfers between devices  17.2 us (10%)
  starting transfers between devices  16.8 us (10%)
  Pallas kernels  14 us (8%)
  local copies, waits for them, and re-layouts  2.02 us (1%)
    all_to_all x6, blocking collectives, exchange(): return lax.all_to_all(chunks, axes, 0, 0, tiled=True)  117 us
    all_to_all x2, waiting for transfers between devices, exchange(): return lax.all_to_all(chunks, axes, 0, 0, tiled=True)  17.2 us
    all_to_all x2, starting transfers between devices, exchange(): return lax.all_to_all(chunks, axes, 0, 0, tiled=True)  16.8 us
    pallas_call x7, Pallas kernels, call(): pl.pallas_call(body, out_shape=outs, in_specs=specs or [VMEM] * len(args)...  14 us
  transfers between devices with their start and end apart: 2, of which 2 were waited for; matrix products, arithmetic and copies ran while one was open for 0% of the time, Pallas kernels for 0%

profile of v1, /device:TPU:1, one launch (start us, length us, event | category | flops | bytes accessed | tf_op | source)
XLA Modules:
  0.0 167.4 jit_solution(13881528957480448996)
XLA Ops:
  0.6 0.0 copy-start
  0.6 0.7 broadcast_in_dim.5
  1.4 18.7 %all_to_all.40 = bf16[16,32,256]{2,1,0:T(8,128)(2,1)S(1)} all-to-all(bf16[16,32,256]{2,1,0:T(8,128)(2,1)S(1)} %broadcast_in_dim.5), channel_id=1, replica_groups=mesh['x'=4,'yh'=2,'core'=2,'yl'=4,'z'=8] {'core','yh','yl'}, dimensions={0} | all-to-all | bytes 524288 | tf_op jit(solution)/shard_map/all_to_all | solution.py:23
  20.1 0.8 broadcast_in_dim.4
  20.9 25.5 %all_to_all.41 = bf16[32,32,256]{2,1,0:T(8,128)(2,1)S(1)} all-to-all(bf16[32,32,256]{2,1,0:T(8,128)(2,1)S(1)} %broadcast_in_dim.4), channel_id=1, replica_groups=mesh['x'=4,'yh'=2,'core'=2,'yl'=4,'z'=8] {'x','z'}, dimensions={0} | all-to-all | bytes 1048576 | tf_op jit(solution)/shard_map/all_to_all | solution.py:23
  46.4 0.0 copy-done
  46.4 1.6 weights.1
  48.1 8.7 %all-to-all-start.2 = ((f32[16,24,128]{2,1,0:T(8,128)}), f32[16,24,128]{2,1,0:T(8,128)S(1)}, u32[]{:S(2)}, u32[]{:S(2)}) async-start(f32[16,24,128]{2,1,0:T(8,128)} %get-tuple-element.10), calls=%async_computation.2 | async-start | bytes 393216 | tf_op jit(solution)/shard_map/all_to_all | solution.py:23
  56.8 8.3 %all-to-all-done.2.in_ref = f32[16,24,128]{2,1,0:T(8,128)S(1)} async-done(((f32[16,24,128]{2,1,0:T(8,128)}), f32[16,24,128]{2,1,0:T(8,128)S(1)}, u32[]{:S(2)}, u32[]{:S(2)}) %all-to-all-start.2) | async-done | bytes 196640 | tf_op jit(solution)/shard_map/all_to_all | solution.py:23
  65.1 2.2 %first_product.1 = (f32[32,16,128]{2,1,0:T(8,128)S(1)}, f32[16,128]{1,0:T(8,128)S(1)}, f32[8,128]{1,0:T(8,128)S(1)}) custom-call(s32[1]{0:T(128)} %bitcast.2.me_ref, f32[1024,512]{1,0:T(8,128)S(1)} %get-tuple-element.9.w_ref, f32[16,24,128]{2,1,0:T(8,128)S(1)} %all-to-all-done.2.in_ref), custom_call_target="tpu_custom_call" | custom-call | tf_op jit(solution)/shard_map/first_product/pallas_call | solution.py:27
  67.3 14.8 %all_to_all.42.in_ref = f32[32,16,128]{2,1,0:T(8,128)S(1)} all-to-all(f32[32,16,128]{2,1,0:T(8,128)S(1)} %get-tuple-element.11), channel_id=1, replica_groups=mesh['x'=4,'yh'=2,'core'=2,'yl'=4,'z'=8] {'x','z'}, dimensions={0} | all-to-all | bytes 524288 | tf_op jit(solution)/shard_map/all_to_all | solution.py:23
  82.1 0.1 first_update.1
  82.2 16.4 %all_to_all.43.in_ref = f32[32,24,128]{2,1,0:T(8,128)S(1)} all-to-all(f32[32,24,128]{2,1,0:T(8,128)S(1)} %first_update.1), channel_id=1, replica_groups=mesh['x'=4,'yh'=2,'core'=2,'yl'=4,'z'=8] {'x','z'}, dimensions={0} | all-to-all | bytes 786432 | tf_op jit(solution)/shard_map/all_to_all | solution.py:23
  98.5 2.4 %second_product.1 = f32[16,48,128]{2,1,0:T(8,128)S(1)} custom-call(f32[1024,512]{1,0:T(8,128)S(1)} %get-tuple-element.9.w_ref, f32[32,24,128]{2,1,0:T(8,128)S(1)} %all_to_all.43.in_ref), custom_call_target="tpu_custom_call" | custom-call | tf_op jit(solution)/shard_map/second_product/pallas_call | solution.py:27
  100.9 22.5 %all_to_all.44.in_ref = f32[16,48,128]{2,1,0:T(8,128)S(1)} all-to-all(f32[16,48,128]{2,1,0:T(8,128)S(1)} %second_product.1), channel_id=1, replica_groups=mesh['x'=4,'yh'=2,'core'=2,'yl'=4,'z'=8] {'core','yh','yl'}, dimensions={0} | all-to-all | bytes 786432 | tf_op jit(solution)/shard_map/all_to_all | solution.py:23
  123.4 3.4 %normalize.1 = (f32[32,64]{1,0:T(8,128)S(1)}, f32[32,32,128]{2,1,0:T(8,128)S(1)}) custom-call(f32[16,48,128]{2,1,0:T(8,128)S(1)} %all_to_all.44.in_ref, f32[16,128]{1,0:T(8,128)S(1)} %get-tuple-element.12.dinv_ref), custom_call_target="tpu_custom_call" | custom-call | tf_op jit(solution)/shard_map/normalize/pallas_call | solution.py:27
  126.8 18.8 %all_to_all.45.in_ref = f32[32,32,128]{2,1,0:T(8,128)S(1)} all-to-all(f32[32,32,128]{2,1,0:T(8,128)S(1)} %get-tuple-element.13), channel_id=1, replica_groups=mesh['x'=4,'yh'=2,'core'=2,'yl'=4,'z'=8] {'x','z'}, dimensions={0} | all-to-all | bytes 1048576 | tf_op jit(solution)/shard_map/all_to_all | solution.py:23
  145.5 0.8 relay.1
  146.3 8.1 %all-to-all-start.7 = ((f32[16,32,128]{2,1,0:T(8,128)}), f32[16,32,128]{2,1,0:T(8,128)S(1)}, u32[]{:S(2)}, u32[]{:S(2)}) async-start(f32[16,32,128]{2,1,0:T(8,128)} %relay.1), calls=%async_computation.7 | async-start | bytes 524288 | tf_op jit(solution)/shard_map/all_to_all | solution.py:23
  154.4 0.5 slice_bitcast_fusion
  154.9 8.9 %all-to-all-done.7.in_ref = f32[16,32,128]{2,1,0:T(8,128)S(1)} async-done(((f32[16,32,128]{2,1,0:T(8,128)}), f32[16,32,128]{2,1,0:T(8,128)S(1)}, u32[]{:S(2)}, u32[]{:S(2)}) %all-to-all-start.7) | async-done | bytes 262176 | tf_op jit(solution)/shard_map/all_to_all | solution.py:23
  163.8 3.6 %orthonormalize.1 = f32[32,64]{1,0:T(8,128)} custom-call(f32[16,32,128]{2,1,0:T(8,128)S(1)} %all-to-all-done.7.in_ref, f32[32,64]{1,0:T(8,128)S(1)} %get-tuple-element.14.update_ref), custom_call_target="tpu_custom_call" | custom-call | tf_op jit(solution)/shard_map/orthonormalize/pallas_call | solution.py:27
Async XLA Ops:
  0.6 45.8 %copy-start = (f32[32,64]{1,0:T(8,128)S(1)}, f32[32,64]{1,0:T(8,128)}, u32[]{:S(2)}) copy-start(f32[32,64]{1,0:T(8,128)} %basis_ref.1) | copy-start | bytes 24580
  48.1 17.0 %all-to-all-start.2 = ((f32[16,24,128]{2,1,0:T(8,128)}), f32[16,24,128]{2,1,0:T(8,128)S(1)}, u32[]{:S(2)}, u32[]{:S(2)}) async-start(f32[16,24,128]{2,1,0:T(8,128)} %get-tuple-element.10), calls=%async_computation.2 | async-start | bytes 393216 | tf_op jit(solution)/shard_map/all_to_all | solution.py:23
  146.3 17.5 %all-to-all-start.7 = ((f32[16,32,128]{2,1,0:T(8,128)}), f32[16,32,128]{2,1,0:T(8,128)S(1)}, u32[]{:S(2)}, u32[]{:S(2)}) async-start(f32[16,32,128]{2,1,0:T(8,128)} %relay.1), calls=%async_computation.7 | async-start | bytes 524288 | tf_op jit(solution)/shard_map/all_to_all | solution.py:23

commit v2 on v1

v2 whole, which is shorter than its diff:
```python
import functools
import math

import jax
import jax.numpy as jnp
from jax import lax
from jax.experimental import pallas as pl
from jax.experimental.pallas import tpu as pltpu
from jax.sharding import Mesh, PartitionSpec as P

AXES = ("x", "yh", "core", "ym", "yl", "zh", "zl")
SIZES = (4, 2, 2, 2, 2, 4, 2)
A_AXES = ("x", "yl", "zl")
B_AXES = ("yh", "ym", "zh")
NA, NB = 16, 16
HIGH = lax.Precision.HIGHEST
F32 = jnp.float32
VMEM = pl.BlockSpec(memory_space=pltpu.VMEM)
SMEM = pl.BlockSpec(memory_space=pltpu.SMEM)


def exchange(chunks, axes):
    return lax.all_to_all(chunks, axes, 0, 0, tiled=True)


def call(body, outs, *args, specs=None, scratch=(), name=None):
    return pl.pallas_call(
        body,
        out_shape=outs,
        in_specs=specs or [VMEM] * len(args),
        out_specs=[VMEM] * len(outs),
        scratch_shapes=list(scratch),
        compiler_params=pltpu.CompilerParams(vmem_limit_bytes=48 * 1024 * 1024),
        name=name,
    )(*args)


def fold(block):
    half = block.shape[0] // 2
    return jnp.concatenate([block[:half], block[half:]], axis=1)


def unfold(packed):
    return jnp.concatenate([packed[:, :64], packed[:, 64:]], axis=0)


def inverse_cholesky(gram):
    n = gram.shape[0]
    tiles = []
    sub = lax.broadcasted_iota(jnp.int32, (8, 128), 0)
    lane = lax.broadcasted_iota(jnp.int32, (8, 128), 1)
    for t in range(n // 8):
        eye = jnp.where(lane == sub + 8 * t + n, 1.0, 0.0).astype(F32)
        left = jnp.concatenate([gram[8 * t : 8 * t + 8], jnp.zeros((8, n), F32)], axis=1)
        tiles.append(left + eye)
    scale = [jnp.ones((8, 128), F32) for _ in tiles]
    group = 4
    for k in range(0, n, group):
        top = k // 8
        cols = [
            {t: jnp.broadcast_to(tiles[t][:, k + j : k + j + 1], (8, 128)) for t in range(top, n // 8)}
            for j in range(group)
        ]
        for j in range(group):
            r = (k + j) % 8
            pivot = jnp.broadcast_to(cols[j][top][r : r + 1], (8, 128))
            scale[top] = jnp.where(sub == r, lax.rsqrt(pivot), scale[top])
            inv = 1.0 / pivot
            row = jnp.broadcast_to(tiles[top][r : r + 1], (8, 128))
            heads = [jnp.broadcast_to(cols[i][top][r : r + 1], (8, 128)) for i in range(j + 1, group)]
            for t in range(top, n // 8):
                factor = cols[j][t] * inv
                if t == top:
                    factor = jnp.where(sub > r, factor, 0.0)
                tiles[t] = tiles[t] - factor * row
                for i in range(j + 1, group):
                    cols[i][t] = cols[i][t] - factor * heads[i - j - 1]
    out = jnp.concatenate([tile * s for tile, s in zip(tiles, scale)], axis=0)
    return out[:, n:]


def total(ref):
    value = ref[0]
    for i in range(1, ref.shape[0]):
        value = value + ref[i]
    return value


def copies_kernel(points_ref, basis_ref, a_ref, b_ref, fold_ref):
    points = points_ref[...]
    for i in range(NA):
        a_ref[i] = points
    for i in range(NB):
        b_ref[i] = points
    fold_ref[...] = fold(basis_ref[...])


def weights_kernel(rows_ref, own_ref, other_ref, basis_ref, w_ref, out_ref):
    rows = rows_ref[...]
    width = rows.shape[1]
    rows32 = rows.astype(F32)
    rows_sq = jnp.sum(rows32 * rows32, axis=1, keepdims=True)
    heads = []
    for half, ref in enumerate((own_ref, other_ref)):
        cols = ref[...]
        count = cols.shape[0]
        dots = lax.dot_general(rows, cols, (((1,), (1,)), ((), ())), preferred_element_type=F32)
        cols32 = cols.astype(F32)
        cols_sq = jnp.sum(cols32 * cols32, axis=1, keepdims=True)
        cols_sq = jnp.transpose(jnp.broadcast_to(cols_sq, (count, 128)))[:1]
        dist = rows_sq + cols_sq - 2.0 * dots
        weights = jnp.exp(-dist / (0.25 * width))
        w_ref[:, half * count : half * count + count] = weights
        sums = jnp.sum(weights, axis=0, keepdims=True)
        heads += [sums[:, 128 * i : 128 * i + 128] for i in range(count // 128)]
    out_ref[:8] = jnp.concatenate(heads, axis=0)
    out_ref[8:] = basis_ref[...]


def share_kernel(core_ref, in_ref, out_ref):
    core = core_ref[0]
    mine, other = in_ref[core], in_ref[1 - core]
    head = mine[:8] + jnp.concatenate([other[4:8], other[:4]], axis=0)
    payload = jnp.concatenate([head, mine[8:], other[8:]], axis=0)
    for i in range(NA):
        out_ref[i] = payload


def first_kernel(me_ref, w_ref, in_ref, part_ref, dinv_ref, deg_ref, column_ref):
    head = in_ref[0, :8]
    for i in range(1, NA):
        head = head + in_ref[i, :8]
    mine = me_ref[0]
    picked = jnp.where(lax.broadcasted_iota(jnp.int32, (8, 128), 0) == mine // 4, head, 0.0)
    picked = jnp.broadcast_to(jnp.sum(picked, axis=0, keepdims=True), (8, 128))
    deg_ref[...] = pltpu.roll(picked, (128 - 32 * (mine % 4)) % 128, 1)
    turned = jnp.transpose(lax.rsqrt(head))
    column = jnp.concatenate([turned[:, i : i + 1] for i in range(8)], axis=0)
    column_ref[...] = jnp.broadcast_to(column[:512], column_ref.shape)
    dinv_ref[...] = fold(column_ref[pl.ds(pl.multiple_of(mine * 32, 32), 32)][:, :64])
    scaled = [unfold(in_ref[i, 8:24]) for i in range(NA)] + [unfold(in_ref[i, 24:]) for i in range(NA)]
    scaled = jnp.concatenate(scaled, axis=0) * column
    part = jnp.dot(w_ref[...], scaled, precision=HIGH, preferred_element_type=F32)
    for i in range(NB):
        part_ref[i] = fold(part[32 * i : 32 * i + 32])


def update_kernel(in_ref, dinv_ref, out_ref):
    dinv = dinv_ref[...]
    update = total(in_ref) * dinv
    lane = lax.broadcasted_iota(jnp.int32, (8, 128), 1)
    rider = jnp.where(lane % 64 < 32, dinv[:8], dinv[8:])
    payload = jnp.concatenate([update, rider], axis=0)
    for i in range(NB):
        out_ref[i] = payload


def outward_kernel(w_ref, in_ref, out_ref, scaled_ref):
    lane = lax.broadcasted_iota(jnp.int32, (8, 128), 1)
    low = lane % 64 < 32
    updates, scaled = [], []
    for i in range(NB):
        update, rider = in_ref[i, :16], in_ref[i, 16:]
        top = jnp.where(low, rider, pltpu.roll(rider, 32, 1))
        bottom = jnp.where(low, pltpu.roll(rider, 96, 1), rider)
        updates.append(update)
        scaled.append(unfold(update * jnp.concatenate([top, bottom], axis=0)))
    packed = jnp.concatenate(updates, axis=0)
    scaled = jnp.concatenate(scaled, axis=0)
    scaled_ref[...] = scaled
    both = lax.dot_general(packed, packed, (((0,), (0,)), ((), ())), precision=HIGH, preferred_element_type=F32)
    gram = fold(both[:64, :64] + both[64:, 64:])
    out_ref[NA] = gram[:16]
    out_ref[NA + 1] = gram[16:]
    half = w_ref.shape[1] // 2
    part = lax.dot_general(
        w_ref[:, half:], scaled, (((0,), (0,)), ((), ())), precision=HIGH, preferred_element_type=F32
    )
    for i in range(NA):
        out_ref[i] = fold(part[32 * i : 32 * i + 32])


def inward_kernel(w_ref, scaled_ref, out_ref):
    half = w_ref.shape[1] // 2
    part = lax.dot_general(
        w_ref[:, :half], scaled_ref[...], (((0,), (0,)), ((), ())), precision=HIGH, preferred_element_type=F32
    )
    for i in range(NA):
        out_ref[i] = fold(part[32 * i : 32 * i + 32])


def join_kernel(sent_ref, came_ref, part_ref, out_ref):
    top = sent_ref[NA] + came_ref[NA]
    bottom = sent_ref[NA + 1] + came_ref[NA + 1]
    for i in range(NA):
        out_ref[i, :16] = part_ref[i] + came_ref[i]
        out_ref[i, 16:32] = top
        out_ref[i, 32:] = bottom


def collect_kernel(in_ref, dinv_ref, out_ref, gram_ref):
    value = total(in_ref)
    update = value[:16] * dinv_ref[...]
    gram_ref[...] = value[16:]
    for i in range(NA):
        out_ref[i] = update


def factor_kernel(gram_ref, inverse_ref):
    inverse_ref[...] = inverse_cholesky(unfold(gram_ref[...]))


def twice(inverse):
    turned = jnp.transpose(inverse)
    none = jnp.zeros_like(turned)
    return jnp.concatenate(
        [jnp.concatenate([turned, none], axis=1), jnp.concatenate([none, turned], axis=1)], axis=0
    )


def normalize_kernel(in_ref, inverse_ref, mine_ref, update_ref, gram_ref):
    both = twice(inverse_ref[...])
    update = jnp.concatenate([in_ref[i] for i in range(NA)], axis=0)
    update = jnp.dot(update, both, precision=HIGH, preferred_element_type=F32)
    gram = lax.dot_general(update, update, (((0,), (0,)), ((), ())), precision=HIGH, preferred_element_type=F32)
    gram_ref[...] = fold(gram[:64, :64] + gram[64:, 64:])
    update_ref[...] = jnp.dot(mine_ref[0], both, precision=HIGH, preferred_element_type=F32)


def spread_kernel(in_ref, out_ref):
    gram = total(in_ref)
    for i in range(NB):
        out_ref[i] = gram


def final_kernel(in_ref, update_ref, out_ref):
    inverse = inverse_cholesky(unfold(total(in_ref)))
    out_ref[...] = lax.dot_general(
        unfold(update_ref[...]), inverse, (((1,), (1,)), ((), ())), precision=HIGH, preferred_element_type=F32
    )


def swap(value):
    return lax.ppermute(value, "core", [(0, 1), (1, 0)])


def per_device(points, basis):
    own, width = points.shape
    shape = lambda *dims: jax.ShapeDtypeStruct(dims, F32)
    core = lax.axis_index("core").astype(jnp.int32).reshape(1)
    me = lax.axis_index(A_AXES).astype(jnp.int32).reshape(1)
    near, far, basis = call(
        copies_kernel,
        [jax.ShapeDtypeStruct((n, own, width), points.dtype) for n in (NA, NB)] + [shape(16, 128)],
        points,
        basis,
        name="copies",
    )
    near = exchange(near, A_AXES).reshape(NA * own, width)
    near_other = swap(near)
    far = exchange(far, B_AXES).reshape(NB * own, width)
    weights, sums = call(
        weights_kernel,
        [shape(NB * own, 2 * NA * own), shape(24, 128)],
        far,
        near,
        near_other,
        basis,
        name="weights",
    )
    sums = lax.all_gather(sums, "core")
    (sums,) = call(share_kernel, [shape(NA, 40, 128)], core, sums, specs=[SMEM, VMEM], name="share")
    sums = exchange(sums, A_AXES)
    part, dinv, degree = call(
        first_kernel,
        [shape(NB, 16, 128), shape(16, 128), shape(8, 128)],
        me,
        weights,
        sums,
        specs=[SMEM, VMEM, VMEM],
        scratch=[pltpu.VMEM((NA * own, 128), F32)],
        name="first_product",
    )
    part = exchange(part, B_AXES)
    (update,) = call(update_kernel, [shape(NB, 24, 128)], part, dinv, name="first_update")
    update = exchange(update, B_AXES)
    sent, scaled = call(
        outward_kernel, [shape(NA + 2, 16, 128), shape(NB * own, 64)], weights, update, name="second_product_other"
    )
    came = swap(sent)
    (part,) = call(inward_kernel, [shape(NA, 16, 128)], weights, scaled, name="second_product_own")
    (part,) = call(join_kernel, [shape(NA, 48, 128)], sent, came, part, name="join")
    part = exchange(part, A_AXES)
    update, gram = call(collect_kernel, [shape(NA, 16, 128), shape(32, 128)], part, dinv, name="collect")
    (inverse,) = call(factor_kernel, [shape(64, 64)], gram, name="factor")
    everyone = exchange(update, A_AXES)
    update, gram = call(normalize_kernel, [shape(16, 128), shape(32, 128)], everyone, inverse, update, name="normalize")
    (gram,) = call(spread_kernel, [shape(NB, 32, 128)], lax.all_gather(gram, "core"), name="spread")
    gram = exchange(gram, B_AXES)
    (out,) = call(final_kernel, [shape(own, 64)], gram, update, name="orthonormalize")
    return (out, degree[0, :own])


def solution(mesh):
    fine = Mesh(mesh.devices.reshape(SIZES), AXES)
    spec = P(AXES)
    return jax.shard_map(
        per_device,
        mesh=fine,
        in_specs=(P(AXES, None), P(AXES, None)),
        out_specs=(P(AXES, None), spec),
        check_vma=False,
    )
```

time: 169 us -> 151 us (0.89)
  blocking collectives: 117 us -> 64.1 us
  starting transfers between devices: 16.8 us -> 34.9 us
  waiting for transfers between devices: 17.2 us -> 31 us
  Pallas kernels: 14 us -> 17.1 us
    all_to_all x6 -> x4, blocking collectives: 117 us -> 55.1 us  [exchange(): return lax.all_to_all(chunks, axes, 0, 0, tiled=True)]
    all_to_all x2 -> x4, waiting for transfers between devices: 17.2 us -> 31 us  [exchange(): return lax.all_to_all(chunks, axes, 0, 0, tiled=True)]
    ppermute x0 -> x2, starting transfers between devices: none -> 10.5 us  [swap(): return lax.ppermute(value, 'core', [(0, 1), (1, 0)])]
    all_gather x0 -> x2, blocking collectives: none -> 9.03 us  [the longest x1 4.97 us: per_device(): sums = lax.all_gather(sums, 'core')]
    all_to_all x2 -> x4, starting transfers between devices: 16.8 us -> 24.3 us  [exchange(): return lax.all_to_all(chunks, axes, 0, 0, tiled=True)]
    pallas_call x7 -> x13, Pallas kernels: 14 us -> 17.1 us  [call(): pl.pallas_call(body, out_shape=outs, in_specs=specs or [VMEM] * len(args)...]
  transfers between devices with their start and end apart: 2 -> 6, of which waited for: 2 -> 4; matrix products, arithmetic and copies ran while one was open for 0% -> 0% of each run, Pallas kernels for 0% -> 3%
where the time goes in v2:
time: 151 us; the launch traced here: 150 us
  blocking collectives  64.1 us (42%)
  starting transfers between devices  34.9 us (23%)
  waiting for transfers between devices  31 us (21%)
  Pallas kernels  17.1 us (11%)
  local copies, waits for them, and re-layouts  1.94 us (1%)
    all_to_all x4, blocking collectives, exchange(): return lax.all_to_all(chunks, axes, 0, 0, tiled=True)  55.1 us
    all_to_all x4, waiting for transfers between devices, exchange(): return lax.all_to_all(chunks, axes, 0, 0, tiled=True)  31 us
    all_to_all x4, starting transfers between devices, exchange(): return lax.all_to_all(chunks, axes, 0, 0, tiled=True)  24.3 us
    pallas_call x13, Pallas kernels, call(): pl.pallas_call(body, out_shape=outs, in_specs=specs or [VMEM] * len(args)...  17.1 us
    ppermute x2, starting transfers between devices, swap(): return lax.ppermute(value, 'core', [(0, 1), (1, 0)])  10.5 us
    all_gather x1, blocking collectives, per_device(): sums = lax.all_gather(sums, 'core')  4.97 us
    all_gather x1, blocking collectives, per_device(): lax.all_gather(gram, 'core')  4.06 us
  transfers between devices with their start and end apart: 6, of which 4 were waited for; matrix products, arithmetic and copies ran while one was open for 0% of the time, Pallas kernels for 3%

profile of v2, /device:TPU:1, one launch (start us, length us, event | category | flops | bytes accessed | tf_op | source)
XLA Modules:
  0.0 149.8 jit_solution(4498598950854724965)
XLA Ops:
  0.6 0.7 copy-done
  1.4 0.7 copy-done.1
  2.1 0.7 copies.1
  2.8 14.4 %all_to_all.40 = bf16[16,32,256]{2,1,0:T(8,128)(2,1)S(1)} all-to-all(bf16[16,32,256]{2,1,0:T(8,128)(2,1)S(1)} %get-tuple-element.17), channel_id=1, replica_groups=mesh['x'=4,'yh'=2,'core'=2,'ym'=2,'yl'=2,'zh'=4,'zl'=2] {'x','yl','zl'}, dimensions={0} | all-to-all | bytes 524288 | tf_op jit(solution)/shard_map/all_to_all | solution.py:23
  17.2 13.8 %all-to-all-start = ((bf16[16,32,256]{2,1,0:T(8,128)(2,1)}), bf16[16,32,256]{2,1,0:T(8,128)(2,1)S(1)}, u32[]{:S(2)}, u32[]{:S(2)}) async-start(bf16[16,32,256]{2,1,0:T(8,128)(2,1)} %get-tuple-element.16), calls=%async_computation | async-start | bytes 524288 | tf_op jit(solution)/shard_map/all_to_all | solution.py:23
  30.9 4.0 %collective-permute-start = (bf16[512,256]{1,0:T(8,128)(2,1)S(1)}, bf16[512,256]{1,0:T(8,128)(2,1)S(1)}, u32[]{:S(2)}, u32[]{:S(2)}) collective-permute-start(bf16[512,256]{1,0:T(8,128)(2,1)S(1)} %bitcast.8), channel_id=1, source_target_pairs={{0,32},{32,0},{1,33},{33,1},{2,34},{34,2},{3,35},{35,3},{4,36},{36... | collective-permute-start | bytes 786440 | tf_op jit(solution)/shard_map/ppermute | solution.py:244
  35.0 7.9 %all-to-all-done = bf16[16,32,256]{2,1,0:T(8,128)(2,1)S(1)} async-done(((bf16[16,32,256]{2,1,0:T(8,128)(2,1)}), bf16[16,32,256]{2,1,0:T(8,128)(2,1)S(1)}, u32[]{:S(2)}, u32[]{:S(2)}) %all-to-all-start) | async-done | bytes 262176 | tf_op jit(solution)/shard_map/all_to_all | solution.py:23
  42.9 0.0 collective-permute-done.other_ref
  42.9 1.0 weights.1
  43.9 5.0 %all-gather = f32[48,128]{1,0:T(8,128)S(1)} all-gather(f32[24,128]{1,0:T(8,128)S(1)} %get-tuple-element.20), channel_id=2, replica_groups=mesh['x'=4,'yh'=2,'core'=2,'ym'=2,'yl'=2,'zh'=4,'zl'=2] {'core'}, dimensions={0}, use_global_device_ids=true | all-gather | bytes 36864 | tf_op jit(solution)/shard_map/all_gather | solution.py:271
  48.9 0.7 share.1
  49.6 3.5 %all-to-all-start.2 = ((f32[16,40,128]{2,1,0:T(8,128)}), f32[16,40,128]{2,1,0:T(8,128)S(1)}, u32[]{:S(2)}, u32[]{:S(2)}) async-start(f32[16,40,128]{2,1,0:T(8,128)} %share.1), calls=%async_computation.2 | async-start | bytes 655360 | tf_op jit(solution)/shard_map/all_to_all | solution.py:23
  53.2 7.5 %all-to-all-done.2.in_ref = f32[16,40,128]{2,1,0:T(8,128)S(1)} async-done(((f32[16,40,128]{2,1,0:T(8,128)}), f32[16,40,128]{2,1,0:T(8,128)S(1)}, u32[]{:S(2)}, u32[]{:S(2)}) %all-to-all-start.2) | async-done | bytes 327712 | tf_op jit(solution)/shard_map/all_to_all | solution.py:23
  60.7 2.2 %first_product.1 = (f32[16,16,128]{2,1,0:T(8,128)S(1)}, f32[16,128]{1,0:T(8,128)S(1)}, f32[8,128]{1,0:T(8,128)S(1)}) custom-call(s32[1]{0:T(128)} %bitcast.2.me_ref, f32[512,1024]{1,0:T(8,128)S(1)} %get-tuple-element.19.w_ref, f32[16,40,128]{2,1,0:T(8,128)S(1)} %all-to-all-done.2.in_ref), custom_call_target="tpu_custom_call" | custom-call | tf_op jit(solution)/shard_map/first_product/pallas_call | solution.py:27
  62.9 15.1 %all_to_all.41.in_ref = f32[16,16,128]{2,1,0:T(8,128)S(1)} all-to-all(f32[16,16,128]{2,1,0:T(8,128)S(1)} %get-tuple-element.21), channel_id=1, replica_groups=mesh['x'=4,'yh'=2,'core'=2,'ym'=2,'yl'=2,'zh'=4,'zl'=2] {'yh','ym','zh'}, dimensions={0} | all-to-all | bytes 262144 | tf_op jit(solution)/shard_map/all_to_all | solution.py:23
  78.0 14.5 %all_to_all.42.in_ref = f32[16,24,128]{2,1,0:T(8,128)S(1)} all-to-all(f32[16,24,128]{2,1,0:T(8,128)S(1)} %first_update.1), channel_id=1, replica_groups=mesh['x'=4,'yh'=2,'core'=2,'ym'=2,'yl'=2,'zh'=4,'zl'=2] {'yh','ym','zh'}, dimensions={0} | all-to-all | bytes 393216 | tf_op jit(solution)/shard_map/all_to_all | solution.py:23
  92.5 1.5 second_product_other.1
  93.9 6.5 %collective-permute-start.1 = (f32[18,16,128]{2,1,0:T(8,128)S(1)}, f32[18,16,128]{2,1,0:T(8,128)S(1)}, u32[]{:S(2)}, u32[]{:S(2)}) collective-permute-start(f32[18,16,128]{2,1,0:T(8,128)S(1)} %get-tuple-element.23.sent_ref), channel_id=1, source_target_pairs={{0,32},{32,0},{1,33},{33,1},{2,34},{34,2},{3,35},{35,3},{4,36},{36... | collective-permute-start | bytes 442376 | tf_op jit(solution)/shard_map/ppermute | solution.py:244
  100.5 1.3 second_product_own.1.part_ref
  101.8 0.0 collective-permute-done.1.came_ref
  101.8 11.1 %all_to_all.43.in_ref = f32[16,48,128]{2,1,0:T(8,128)S(1)} all-to-all(f32[16,48,128]{2,1,0:T(8,128)S(1)} %join.1), channel_id=1, replica_groups=mesh['x'=4,'yh'=2,'core'=2,'ym'=2,'yl'=2,'zh'=4,'zl'=2] {'x','yl','zl'}, dimensions={0} | all-to-all | bytes 786432 | tf_op jit(solution)/shard_map/all_to_all | solution.py:23
  112.9 0.7 collect.1
  113.6 3.5 %all-to-all-start.6 = ((f32[16,16,128]{2,1,0:T(8,128)}), f32[16,16,128]{2,1,0:T(8,128)S(1)}, u32[]{:S(2)}, u32[]{:S(2)}) async-start(f32[16,16,128]{2,1,0:T(8,128)} %get-tuple-element.25.mine_ref), calls=%async_computation.6 | async-start | bytes 262144 | tf_op jit(solution)/shard_map/all_to_all | solution.py:23
  117.1 2.8 %factor.1.inverse_ref = f32[64,64]{1,0:T(8,128)S(1)} custom-call(f32[32,128]{1,0:T(8,128)S(1)} %get-tuple-element.26.gram_ref), custom_call_target="tpu_custom_call" | custom-call | tf_op jit(solution)/shard_map/factor/pallas_call | solution.py:27
  119.9 3.4 %all-to-all-done.6.in_ref = f32[16,16,128]{2,1,0:T(8,128)S(1)} async-done(((f32[16,16,128]{2,1,0:T(8,128)}), f32[16,16,128]{2,1,0:T(8,128)S(1)}, u32[]{:S(2)}, u32[]{:S(2)}) %all-to-all-start.6) | async-done | bytes 131104 | tf_op jit(solution)/shard_map/all_to_all | solution.py:23
  123.3 1.8 %normalize.1 = (f32[16,128]{1,0:T(8,128)S(1)}, f32[32,128]{1,0:T(8,128)S(1)}) custom-call(f32[16,16,128]{2,1,0:T(8,128)S(1)} %all-to-all-done.6.in_ref, f32[64,64]{1,0:T(8,128)S(1)} %factor.1.inverse_ref, f32[16,16,128]{2,1,0:T(8,128)} %get-tuple-element.25.mine_ref), custom_call_target="tpu_custom_call" | custom-call | tf_op jit(solution)/shard_map/normalize/pallas_call | solution.py:27
  125.2 4.1 %all-gather.1 = f32[64,128]{1,0:T(8,128)S(1)} all-gather(f32[32,128]{1,0:T(8,128)S(1)} %get-tuple-element.27), channel_id=3, replica_groups=mesh['x'=4,'yh'=2,'core'=2,'ym'=2,'yl'=2,'zh'=4,'zl'=2] {'core'}, dimensions={0}, use_global_device_ids=true | all-gather | bytes 49152 | tf_op jit(solution)/shard_map/all_gather | solution.py:298
  129.2 0.7 spread.1
  130.0 3.5 %all-to-all-start.7 = ((f32[16,32,128]{2,1,0:T(8,128)}), f32[16,32,128]{2,1,0:T(8,128)S(1)}, u32[]{:S(2)}, u32[]{:S(2)}) async-start(f32[16,32,128]{2,1,0:T(8,128)} %spread.1), calls=%async_computation.7 | async-start | bytes 524288 | tf_op jit(solution)/shard_map/all_to_all | solution.py:23
  133.5 0.5 slice_bitcast_fusion
  134.0 12.2 %all-to-all-done.7.in_ref = f32[16,32,128]{2,1,0:T(8,128)S(1)} async-done(((f32[16,32,128]{2,1,0:T(8,128)}), f32[16,32,128]{2,1,0:T(8,128)S(1)}, u32[]{:S(2)}, u32[]{:S(2)}) %all-to-all-start.7) | async-done | bytes 262176 | tf_op jit(solution)/shard_map/all_to_all | solution.py:23
  146.2 3.6 %orthonormalize.1 = f32[32,64]{1,0:T(8,128)} custom-call(f32[16,32,128]{2,1,0:T(8,128)S(1)} %all-to-all-done.7.in_ref, f32[16,128]{1,0:T(8,128)S(1)} %get-tuple-element.28.update_ref), custom_call_target="tpu_custom_call" | custom-call | tf_op jit(solution)/shard_map/orthonormalize/pallas_call | solution.py:27
  (4 shorter events, 0.1 us)
Async XLA Ops:
  0.6 0.7 copy-start
  1.3 0.7 copy-start.1
  17.2 25.7 %all-to-all-start = ((bf16[16,32,256]{2,1,0:T(8,128)(2,1)}), bf16[16,32,256]{2,1,0:T(8,128)(2,1)S(1)}, u32[]{:S(2)}, u32[]{:S(2)}) async-start(bf16[16,32,256]{2,1,0:T(8,128)(2,1)} %get-tuple-element.16), calls=%async_computation | async-start | bytes 524288 | tf_op jit(solution)/shard_map/all_to_all | solution.py:23
  30.9 12.0 %collective-permute-start = (bf16[512,256]{1,0:T(8,128)(2,1)S(1)}, bf16[512,256]{1,0:T(8,128)(2,1)S(1)}, u32[]{:S(2)}, u32[]{:S(2)}) collective-permute-start(bf16[512,256]{1,0:T(8,128)(2,1)S(1)} %bitcast.8), channel_id=1, source_target_pairs={{0,32},{32,0},{1,33},{33,1},{2,34},{34,2},{3,35},{35,3},{4,36},{36... | collective-permute-start | bytes 786440 | tf_op jit(solution)/shard_map/ppermute | solution.py:244
  49.6 11.0 %all-to-all-start.2 = ((f32[16,40,128]{2,1,0:T(8,128)}), f32[16,40,128]{2,1,0:T(8,128)S(1)}, u32[]{:S(2)}, u32[]{:S(2)}) async-start(f32[16,40,128]{2,1,0:T(8,128)} %share.1), calls=%async_computation.2 | async-start | bytes 655360 | tf_op jit(solution)/shard_map/all_to_all | solution.py:23
  93.9 7.8 %collective-permute-start.1 = (f32[18,16,128]{2,1,0:T(8,128)S(1)}, f32[18,16,128]{2,1,0:T(8,128)S(1)}, u32[]{:S(2)}, u32[]{:S(2)}) collective-permute-start(f32[18,16,128]{2,1,0:T(8,128)S(1)} %get-tuple-element.23.sent_ref), channel_id=1, source_target_pairs={{0,32},{32,0},{1,33},{33,1},{2,34},{34,2},{3,35},{35,3},{4,36},{36... | collective-permute-start | bytes 442376 | tf_op jit(solution)/shard_map/ppermute | solution.py:244
  113.6 9.7 %all-to-all-start.6 = ((f32[16,16,128]{2,1,0:T(8,128)}), f32[16,16,128]{2,1,0:T(8,128)S(1)}, u32[]{:S(2)}, u32[]{:S(2)}) async-start(f32[16,16,128]{2,1,0:T(8,128)} %get-tuple-element.25.mine_ref), calls=%async_computation.6 | async-start | bytes 262144 | tf_op jit(solution)/shard_map/all_to_all | solution.py:23
  130.0 16.3 %all-to-all-start.7 = ((f32[16,32,128]{2,1,0:T(8,128)}), f32[16,32,128]{2,1,0:T(8,128)S(1)}, u32[]{:S(2)}, u32[]{:S(2)}) async-start(f32[16,32,128]{2,1,0:T(8,128)} %spread.1), calls=%async_computation.7 | async-start | bytes 524288 | tf_op jit(solution)/shard_map/all_to_all | solution.py:23

commit v3 on v1

v3 whole, which is shorter than its diff:
```python
import jax
import jax.numpy as jnp
from jax import lax
from jax.experimental import pallas as pl
from jax.experimental.pallas import tpu as pltpu
from jax.sharding import Mesh, PartitionSpec as P

AXES = ("x", "yh", "core", "ym", "yl", "zh", "zl")
SIZES = (4, 2, 2, 2, 2, 4, 2)
A_AXES = ("x", "yl", "zl")
B_AXES = ("yh", "ym", "zh")
NA, NB = 16, 16
OWN, HALF, LINE = 32, 16, 256
HIGH = lax.Precision.HIGHEST
F32, BF16 = jnp.float32, jnp.bfloat16
VMEM = pl.BlockSpec(memory_space=pltpu.VMEM)
ANY = pl.BlockSpec(memory_space=pl.ANY)


def exchange(chunks, axes):
    return lax.all_to_all(chunks, axes, 0, 0, tiled=True)


def swap(value):
    return lax.ppermute(value, "core", [(0, 1), (1, 0)])


def call(body, outs, *args, specs=None, scratch=(), name=None):
    return pl.pallas_call(
        body,
        out_shape=outs,
        in_specs=specs or [VMEM] * len(args),
        out_specs=[VMEM] * len(outs),
        scratch_shapes=list(scratch),
        compiler_params=pltpu.CompilerParams(vmem_limit_bytes=48 * 1024 * 1024),
        name=name,
    )(*args)


def fold(block):
    half = block.shape[0] // 2
    return jnp.concatenate([block[:half], block[half:]], axis=1)


def unfold(packed):
    return jnp.concatenate([packed[:, :64], packed[:, 64:]], axis=0)


def total(ref):
    value = ref[0]
    for i in range(1, ref.shape[0]):
        value = value + ref[i]
    return value


def split(value):
    high = value.astype(BF16)
    rest = value - high.astype(F32)
    middle = rest.astype(BF16)
    return high, middle, (rest - middle.astype(F32)).astype(BF16)


def turn_out(packed):
    turned = jnp.transpose(packed)
    return jnp.concatenate([turned[:64], turned[64:]], axis=1)


def product(scaled, weights, axis):
    high, middle, low = (ref[...] for ref in weights)
    over = lambda left, right: lax.dot_general(
        left, right, (((1,), (axis,)), ((), ())), preferred_element_type=F32
    )
    top = over(scaled, high)
    part = over(scaled[:128], middle)
    return top[:64] + (top[64:128] + part[:64]) + (top[128:] + part[64:] + over(scaled[:64], low))


def turn_in(part):
    return jnp.transpose(jnp.concatenate([part[:, :LINE], part[:, LINE:]], axis=0))


def gram_of(packed):
    both = lax.dot_general(packed, packed, (((0,), (0,)), ((), ())), precision=HIGH, preferred_element_type=F32)
    return both[:64, :64] + both[64:, 64:]


def shrink(gram):
    blocks = gram[:32, :32], gram[32:, :32], gram[32:, 32:]
    rows = [jnp.concatenate([block[8 * j : 8 * j + 8] for j in range(4)], axis=1) for block in blocks]
    return jnp.concatenate(rows, axis=0)


def grow(packed):
    blocks = [
        jnp.concatenate([packed[8 * i : 8 * i + 8, 32 * j : 32 * j + 32] for j in range(4)], axis=0) for i in range(3)
    ]
    lower = jnp.concatenate(
        [
            jnp.concatenate([blocks[0], jnp.zeros((32, 32), F32)], axis=1),
            jnp.concatenate([blocks[1], blocks[2]], axis=1),
        ],
        axis=0,
    )
    return jnp.where(lax.broadcasted_iota(jnp.int32, (64, 64), 1) < 32, lower, jnp.transpose(lower))


def inverse_cholesky(gram):
    n = gram.shape[0]
    tiles = []
    sub = lax.broadcasted_iota(jnp.int32, (8, 128), 0)
    lane = lax.broadcasted_iota(jnp.int32, (8, 128), 1)
    for t in range(n // 8):
        eye = jnp.where(lane == sub + 8 * t + n, 1.0, 0.0).astype(F32)
        left = jnp.concatenate([gram[8 * t : 8 * t + 8], jnp.zeros((8, n), F32)], axis=1)
        tiles.append(left + eye)
    scale = [jnp.ones((8, 128), F32) for _ in tiles]
    for top in range(n // 8):
        cols = [
            {t: jnp.broadcast_to(tiles[t][:, 8 * top + j : 8 * top + j + 1], (8, 128)) for t in range(top, n // 8)}
            for j in range(8)
        ]
        for r in range(8):
            pivot = jnp.broadcast_to(cols[r][top][r : r + 1], (8, 128))
            scale[top] = jnp.where(sub == r, lax.rsqrt(pivot), scale[top])
            inv = 1.0 / pivot
            row = jnp.broadcast_to(tiles[top][r : r + 1], (8, 128))
            heads = [jnp.broadcast_to(cols[i][top][r : r + 1], (8, 128)) for i in range(r + 1, 8)]
            for t in range(top, n // 8):
                factor = cols[r][t] * inv
                if t == top:
                    factor = jnp.where(sub > r, factor, 0.0)
                tiles[t] = tiles[t] - factor * row
                for i in range(r + 1, 8):
                    cols[i][t] = cols[i][t] - factor * heads[i - r - 1]
    out = jnp.concatenate([tile * s for tile, s in zip(tiles, scale)], axis=0)
    return out[:, n:]


def near_kernel(points_ref, out_ref):
    points = points_ref[...]
    for i in range(NA):
        out_ref[i] = points


def far_kernel(points_ref, basis_ref, after_ref, out_ref, fold_ref):
    points = points_ref[...]
    for i in range(NB):
        out_ref[i] = points
    fold_ref[...] = fold(basis_ref[...])


def affinity(far_ref, near_ref, out_refs):
    rows, cols = (
        jnp.concatenate([ref[i, h : h + HALF] for h in (0, HALF) for i in range(ref.shape[0])], axis=0)
        for ref in (far_ref, near_ref)
    )
    count, width = cols.shape
    dots = lax.dot_general(rows, cols, (((1,), (1,)), ((), ())), preferred_element_type=F32)
    rows32, cols32 = rows.astype(F32), cols.astype(F32)
    rows_sq = jnp.sum(rows32 * rows32, axis=1, keepdims=True)
    cols_sq = jnp.sum(cols32 * cols32, axis=1, keepdims=True)
    cols_sq = jnp.transpose(jnp.broadcast_to(cols_sq, (count, 128)))[:1]
    dist = rows_sq + cols_sq - 2.0 * dots
    weights = jnp.exp(-dist / (0.25 * width))
    for ref, value in zip(out_refs, split(weights)):
        ref[...] = value
    sums = jnp.sum(weights, axis=0, keepdims=True)
    return jnp.concatenate([sums[:, 128 * i : 128 * i + 128] for i in range(count // 128)], axis=0)


def own_weights_kernel(far_ref, near_ref, high_ref, middle_ref, low_ref, sums_ref):
    sums_ref[:4] = affinity(far_ref, near_ref, (high_ref, middle_ref, low_ref))


def other_weights_kernel(far_ref, near_ref, sums_ref, basis_ref, high_ref, middle_ref, low_ref, out_ref):
    sums = affinity(far_ref, near_ref, (high_ref, middle_ref, low_ref))
    out_ref[:8] = jnp.concatenate([sums_ref[:4], sums], axis=0)
    out_ref[8:] = basis_ref[...]


def share_kernel(in_ref, out_ref):
    core = lax.axis_index("core")
    mine, other = in_ref[core], in_ref[1 - core]
    head = mine[:8] + jnp.concatenate([other[4:8], other[:4]], axis=0)
    payload = jnp.concatenate([head, mine[8:], other[8:]], axis=0)
    for i in range(NA):
        out_ref[i] = payload


def first_kernel(*refs):
    own_refs, other_refs = refs[:3], refs[3:6]
    in_ref, part_ref, dinv_ref, deg_ref, dinvs_ref = refs[6:]
    head = in_ref[0, :8]
    for i in range(1, NA):
        head = head + in_ref[i, :8]
    mine = lax.axis_index(A_AXES)
    sub = lax.broadcasted_iota(jnp.int32, (8, 128), 0)
    lane = lax.broadcasted_iota(jnp.int32, (8, 128), 1)
    lines = []
    for h in range(2):
        line = jnp.sum(jnp.where(sub == 2 * h + mine // 8, head, 0.0), axis=0, keepdims=True)
        lines.append(pltpu.roll(jnp.broadcast_to(line, (8, 128)), (128 + HALF * h - HALF * (mine % 8)) % 128, 1))
    deg_ref[...] = jnp.where(lane < HALF, lines[0], lines[1])[0, :OWN]
    turned = jnp.transpose(lax.rsqrt(head))
    first = lax.broadcasted_iota(jnp.int32, (LINE, 128), 1) < 64
    scaled = []
    for side in range(2):
        columns = [
            jnp.concatenate([turned[:, 4 * side + 2 * h + i : 4 * side + 2 * h + i + 1] for i in range(2)], axis=0)
            for h in range(2)
        ]
        dinv = jnp.where(first, jnp.broadcast_to(columns[0], (LINE, 128)), jnp.broadcast_to(columns[1], (LINE, 128)))
        if side == 0:
            dinvs_ref[...] = dinv
        packed = jnp.concatenate([in_ref[i, 8 + HALF * side : 24 + HALF * side] for i in range(NA)], axis=0)
        scaled.append(turn_out(packed * dinv))
    dinv_ref[...] = dinvs_ref[pl.ds(pl.multiple_of(mine * HALF, HALF), HALF)]
    part = sum(
        product(jnp.concatenate(split(values), axis=0), weights, 1)
        for values, weights in zip(scaled, (own_refs, other_refs))
    )
    part = turn_in(part)
    for i in range(NB):
        part_ref[i] = part[HALF * i : HALF * i + HALF]


def update_kernel(in_ref, dinv_ref, out_ref):
    dinv = dinv_ref[...]
    update = total(in_ref) * dinv
    lane = lax.broadcasted_iota(jnp.int32, (8, 128), 1)
    rider = jnp.where(lane % 64 < 32, dinv[:8], dinv[8:])
    payload = jnp.concatenate([update, rider], axis=0)
    for i in range(NB):
        out_ref[i] = payload


def outward_kernel(high_ref, middle_ref, low_ref, in_ref, out_ref, scaled_ref):
    lane = lax.broadcasted_iota(jnp.int32, (8, 128), 1)
    low = lane % 64 < 32
    updates, scaled = [], []
    for i in range(NB):
        update, rider = in_ref[i, :16], in_ref[i, 16:]
        top = jnp.where(low, rider, pltpu.roll(rider, 32, 1))
        bottom = jnp.where(low, pltpu.roll(rider, 96, 1), rider)
        updates.append(update)
        scaled.append(update * jnp.concatenate([top, bottom], axis=0))
    scaled = jnp.concatenate(split(turn_out(jnp.concatenate(scaled, axis=0))), axis=0)
    scaled_ref[...] = scaled
    out_ref[LINE:] = shrink(gram_of(jnp.concatenate(updates, axis=0)))
    out_ref[:LINE] = turn_in(product(scaled, (high_ref, middle_ref, low_ref), 0))


def inward_kernel(high_ref, middle_ref, low_ref, scaled_ref, out_ref):
    out_ref[...] = turn_in(product(scaled_ref[...], (high_ref, middle_ref, low_ref), 0))


def join_kernel(sent_ref, came_ref, part_ref, out_ref):
    gram = sent_ref[LINE:] + came_ref[LINE:]
    for i in range(NA):
        here = slice(HALF * i, HALF * i + HALF)
        out_ref[i, :HALF] = part_ref[here] + came_ref[here]
        out_ref[i, HALF:] = gram


def collect_kernel(in_ref, dinv_ref, out_ref, gram_ref):
    value = total(in_ref)
    update = value[:HALF] * dinv_ref[...]
    gram_ref[...] = value[HALF:]
    for i in range(NA):
        out_ref[i] = update


def factor_kernel(gram_ref, inverse_ref):
    turned = jnp.transpose(inverse_cholesky(grow(gram_ref[...])))
    none = jnp.zeros_like(turned)
    inverse_ref[:64] = jnp.concatenate([turned, none], axis=1)
    inverse_ref[64:] = jnp.concatenate([none, turned], axis=1)


def normalize_kernel(in_ref, inverse_ref, update_ref, out_ref, updates_ref):
    inverse = inverse_ref[...]
    update = jnp.concatenate([in_ref[i] for i in range(NA)], axis=0)
    update = jnp.dot(update, inverse, precision=HIGH, preferred_element_type=F32)
    updates_ref[...] = update
    mine = lax.axis_index(A_AXES)
    update_ref[...] = updates_ref[pl.ds(pl.multiple_of(mine * HALF, HALF), HALF)]
    gram = shrink(gram_of(update))
    for i in range(NB):
        out_ref[i] = gram


def relay_kernel(in_ref, out_ref):
    out_ref[...] = total(in_ref)


def final_kernel(in_ref, update_ref, out_ref):
    inverse = inverse_cholesky(grow(total(in_ref)))
    out_ref[...] = lax.dot_general(
        unfold(update_ref[...]), inverse, (((1,), (1,)), ((), ())), precision=HIGH, preferred_element_type=F32
    )


def per_device(points, basis):
    own, width = points.shape
    shape = lambda *dims, dtype=F32: jax.ShapeDtypeStruct(dims, dtype)
    (near,) = call(near_kernel, [shape(NA, own, width, dtype=BF16)], points, name="near_copies")
    near = exchange(near, A_AXES)
    other = swap(near)
    far, basis = call(
        far_kernel,
        [shape(NB, own, width, dtype=BF16), shape(HALF, 128)],
        points,
        basis,
        near,
        specs=[VMEM, VMEM, ANY],
        name="far_copies",
    )
    far = exchange(far, B_AXES)
    parts = [shape(NB * own, NA * own, dtype=BF16)] * 3
    *own_weights, sums = call(own_weights_kernel, parts + [shape(8, 128)], far, near, name="own_weights")
    *other_weights, sums = call(
        other_weights_kernel, parts + [shape(8 + HALF, 128)], far, other, sums, basis, name="other_weights"
    )
    sums = lax.all_gather(sums, "core")
    (sums,) = call(share_kernel, [shape(NA, 8 + 2 * HALF, 128)], sums, name="share")
    sums = exchange(sums, A_AXES)
    part, dinv, degree = call(
        first_kernel,
        [shape(NB, HALF, 128), shape(HALF, 128), shape(own)],
        *own_weights,
        *other_weights,
        sums,
        scratch=[pltpu.VMEM((LINE, 128), F32)],
        name="first_product",
    )
    part = exchange(part, B_AXES)
    (update,) = call(update_kernel, [shape(NB, HALF + 8, 128)], part, dinv, name="first_update")
    update = exchange(update, B_AXES)
    sent, scaled = call(
        outward_kernel,
        [shape(LINE + 24, 128), shape(192, NB * own, dtype=BF16)],
        *other_weights,
        update,
        name="second_product_other",
    )
    came = swap(sent)
    (part,) = call(inward_kernel, [shape(LINE, 128)], *own_weights, scaled, name="second_product_own")
    (part,) = call(join_kernel, [shape(NA, HALF + 24, 128)], sent, came, part, name="join")
    part = exchange(part, A_AXES)
    update, gram = call(collect_kernel, [shape(NA, HALF, 128), shape(24, 128)], part, dinv, name="collect")
    (inverse,) = call(factor_kernel, [shape(128, 128)], gram, name="factor")
    everyone = exchange(update, A_AXES)
    update, gram = call(
        normalize_kernel,
        [shape(HALF, 128), shape(NB, 24, 128)],
        everyone,
        inverse,
        scratch=[pltpu.VMEM((LINE, 128), F32)],
        name="normalize",
    )
    (gram,) = call(relay_kernel, [shape(24, 128)], exchange(gram, B_AXES), name="relay")
    (out,) = call(final_kernel, [shape(own, 64)], lax.all_gather(gram, "core"), update, name="orthonormalize")
    return (out, degree)


def solution(mesh):
    fine = Mesh(mesh.devices.reshape(SIZES), AXES)
    return jax.shard_map(
        per_device,
        mesh=fine,
        in_specs=(P(AXES, None), P(AXES, None)),
        out_specs=(P(AXES, None), P(AXES)),
        check_vma=False,
    )
```

time: 169 us -> 145 us (0.86)
  blocking collectives: 117 us -> 90.6 us
  starting transfers between devices: 16.8 us -> 28.2 us
  waiting for transfers between devices: 17.2 us -> 12.5 us
  Pallas kernels: 14 us -> 12 us
    all_to_all x6, blocking collectives: 117 us -> 79.5 us  [exchange(): return lax.all_to_all(chunks, axes, 0, 0, tiled=True)]
    all_gather x0 -> x2, blocking collectives: none -> 11 us  [the longest x1 6.05 us: per_device(): lax.all_gather(gram, 'core')]
    ppermute x0 -> x2, starting transfers between devices: none -> 10.7 us  [swap(): return lax.ppermute(value, 'core', [(0, 1), (1, 0)])]
    all_to_all x2, waiting for transfers between devices: 17.2 us -> 12 us  [exchange(): return lax.all_to_all(chunks, axes, 0, 0, tiled=True)]
    pallas_call x7 -> x15, Pallas kernels: 14 us -> 12 us  [call(): pl.pallas_call(body, out_shape=outs, in_specs=specs or [VMEM] * len(args)...]
  transfers between devices with their start and end apart: 2 -> 4, of which waited for: 2 -> 3; matrix products, arithmetic and copies ran while one was open for 0% -> 0% of each run, Pallas kernels for 0% -> 2%
where the time goes in v3:
time: 145 us
  blocking collectives  90.6 us (62%)
  starting transfers between devices  28.2 us (19%)
  waiting for transfers between devices  12.5 us (9%)
  Pallas kernels  12 us (8%)
    all_to_all x6, blocking collectives, exchange(): return lax.all_to_all(chunks, axes, 0, 0, tiled=True)  79.5 us
    all_to_all x2, starting transfers between devices, exchange(): return lax.all_to_all(chunks, axes, 0, 0, tiled=True)  17.5 us
    all_to_all x2, waiting for transfers between devices, exchange(): return lax.all_to_all(chunks, axes, 0, 0, tiled=True)  12 us
    pallas_call x15, Pallas kernels, call(): pl.pallas_call(body, out_shape=outs, in_specs=specs or [VMEM] * len(args)...  12 us
    ppermute x2, starting transfers between devices, swap(): return lax.ppermute(value, 'core', [(0, 1), (1, 0)])  10.7 us
    all_gather x1, blocking collectives, per_device(): lax.all_gather(gram, 'core')  6.05 us
    all_gather x1, blocking collectives, per_device(): sums = lax.all_gather(sums, 'core')  4.98 us
  transfers between devices with their start and end apart: 4, of which 3 were waited for; matrix products, arithmetic and copies ran while one was open for 0% of the time, Pallas kernels for 2%

profile of v3, /device:TPU:1, one launch (start us, length us, event | category | flops | bytes accessed | tf_op | source)
XLA Modules:
  0.0 144.8 jit_solution(717962389733151945)
XLA Ops:
  0.6 0.0 copy-start
  0.6 0.7 copy-done
  1.4 0.0 copy-start.1
  1.4 14.4 %all_to_all.40.after_ref.near_ref = bf16[16,32,256]{2,1,0:T(8,128)(2,1)S(1)} all-to-all(bf16[16,32,256]{2,1,0:T(8,128)(2,1)S(1)} %near_copies.1), channel_id=1, replica_groups=mesh['x'=4,'yh'=2,'core'=2,'ym'=2,'yl'=2,'zh'=4,'zl'=2] {'x','yl','zl'}, dimensions={0} | all-to-all | bytes 524288 | tf_op jit(solution)/shard_map/all_to_all | solution.py:21
  15.8 0.0 copy-done.1
  15.8 0.7 far_copies.1
  16.5 13.8 %all-to-all-start.1 = ((bf16[16,32,256]{2,1,0:T(8,128)(2,1)}), bf16[16,32,256]{2,1,0:T(8,128)(2,1)S(1)}, u32[]{:S(2)}, u32[]{:S(2)}) async-start(bf16[16,32,256]{2,1,0:T(8,128)(2,1)} %get-tuple-element.21), calls=%async_computation.1 | async-start | bytes 524288 | tf_op jit(solution)/shard_map/all_to_all | solution.py:21
  30.3 4.0 %collective-permute-start = (bf16[16,32,256]{2,1,0:T(8,128)(2,1)S(1)}, bf16[16,32,256]{2,1,0:T(8,128)(2,1)S(1)}, u32[]{:S(2)}, u32[]{:S(2)}) collective-permute-start(bf16[16,32,256]{2,1,0:T(8,128)(2,1)S(1)} %all_to_all.40.after_ref.near_ref), channel_id=1, source_target_pairs={{0,32},{32,0},{1,33},{33,1},{2,34},{34,2},{3,35},{35,3},{4,36},{36... | collective-permute-start | bytes 786440 | tf_op jit(solution)/shard_map/ppermute | solution.py:25
  34.3 7.9 %all-to-all-done.1.far_ref = bf16[16,32,256]{2,1,0:T(8,128)(2,1)S(1)} async-done(((bf16[16,32,256]{2,1,0:T(8,128)(2,1)}), bf16[16,32,256]{2,1,0:T(8,128)(2,1)S(1)}, u32[]{:S(2)}, u32[]{:S(2)}) %all-to-all-start.1) | async-done | bytes 262176 | tf_op jit(solution)/shard_map/all_to_all | solution.py:21
  42.2 0.9 own_weights.1
  43.1 0.0 collective-permute-done.near_ref
  43.1 0.9 other_weights.1
  43.9 5.0 %all-gather = f32[48,128]{1,0:T(8,128)S(1)} all-gather(f32[24,128]{1,0:T(8,128)S(1)} %get-tuple-element.30), channel_id=2, replica_groups=mesh['x'=4,'yh'=2,'core'=2,'ym'=2,'yl'=2,'zh'=4,'zl'=2] {'core'}, dimensions={0}, use_global_device_ids=true | all-gather | bytes 36864 | tf_op jit(solution)/shard_map/all_gather | solution.py:324
  49.0 10.0 %all_to_all.41.refs_6_ = f32[16,40,128]{2,1,0:T(8,128)S(1)} all-to-all(f32[16,40,128]{2,1,0:T(8,128)S(1)} %share.1), channel_id=1, replica_groups=mesh['x'=4,'yh'=2,'core'=2,'ym'=2,'yl'=2,'zh'=4,'zl'=2] {'x','yl','zl'}, dimensions={0} | all-to-all | bytes 655360 | tf_op jit(solution)/shard_map/all_to_all | solution.py:21
  58.9 1.8 %first_product.1 = (f32[16,16,128]{2,1,0:T(8,128)S(1)}, f32[16,128]{1,0:T(8,128)S(1)}, f32[32]{0:T(128)}) custom-call(bf16[512,512]{1,0:T(8,128)(2,1)S(1)} %get-tuple-element.27.refs_0_.high_ref, bf16[512,512]{1,0:T(8,128)(2,1)S(1)} %get-tuple-element.28.refs_1_.middle_ref, bf16[512,512]{1,0:T(8,128)(2,1)S(1)} %get-tuple-element.29.refs_2_.low_ref, ...), custom_call_target="tpu_custom_call" | custom-call | tf_op jit(solution)/shard_map/first_product/pallas_call | solution.py:29
  60.8 15.5 %all_to_all.42.in_ref = f32[16,16,128]{2,1,0:T(8,128)S(1)} all-to-all(f32[16,16,128]{2,1,0:T(8,128)S(1)} %get-tuple-element.31), channel_id=1, replica_groups=mesh['x'=4,'yh'=2,'core'=2,'ym'=2,'yl'=2,'zh'=4,'zl'=2] {'yh','ym','zh'}, dimensions={0} | all-to-all | bytes 262144 | tf_op jit(solution)/shard_map/all_to_all | solution.py:21
  76.2 14.5 %all_to_all.43.in_ref = f32[16,24,128]{2,1,0:T(8,128)S(1)} all-to-all(f32[16,24,128]{2,1,0:T(8,128)S(1)} %first_update.1), channel_id=1, replica_groups=mesh['x'=4,'yh'=2,'core'=2,'ym'=2,'yl'=2,'zh'=4,'zl'=2] {'yh','ym','zh'}, dimensions={0} | all-to-all | bytes 393216 | tf_op jit(solution)/shard_map/all_to_all | solution.py:21
  90.8 0.7 second_product_other.1
  91.5 6.7 %collective-permute-start.1 = (f32[280,128]{1,0:T(8,128)S(1)}, f32[280,128]{1,0:T(8,128)S(1)}, u32[]{:S(2)}, u32[]{:S(2)}) collective-permute-start(f32[280,128]{1,0:T(8,128)S(1)} %get-tuple-element.33.sent_ref), channel_id=1, source_target_pairs={{0,32},{32,0},{1,33},{33,1},{2,34},{34,2},{3,35},{35,3},{4,36},{36... | collective-permute-start | bytes 430088 | tf_op jit(solution)/shard_map/ppermute | solution.py:25
  98.1 0.5 second_product_own.1.part_ref
  98.6 0.5 collective-permute-done.1.came_ref
  99.2 10.0 %all_to_all.44.in_ref = f32[16,40,128]{2,1,0:T(8,128)S(1)} all-to-all(f32[16,40,128]{2,1,0:T(8,128)S(1)} %join.1), channel_id=1, replica_groups=mesh['x'=4,'yh'=2,'core'=2,'ym'=2,'yl'=2,'zh'=4,'zl'=2] {'x','yl','zl'}, dimensions={0} | all-to-all | bytes 655360 | tf_op jit(solution)/shard_map/all_to_all | solution.py:21
  109.2 0.7 collect.1
  109.8 3.8 %all-to-all-start.6 = ((f32[16,16,128]{2,1,0:T(8,128)}), f32[16,16,128]{2,1,0:T(8,128)S(1)}, u32[]{:S(2)}, u32[]{:S(2)}) async-start(f32[16,16,128]{2,1,0:T(8,128)} %get-tuple-element.35), calls=%async_computation.6 | async-start | bytes 262144 | tf_op jit(solution)/shard_map/all_to_all | solution.py:21
  113.6 2.1 %factor.1.inverse_ref = f32[128,128]{1,0:T(8,128)S(1)} custom-call(f32[24,128]{1,0:T(8,128)S(1)} %get-tuple-element.36.gram_ref), custom_call_target="tpu_custom_call" | custom-call | tf_op jit(solution)/shard_map/factor/pallas_call | solution.py:29
  115.8 4.1 %all-to-all-done.6.in_ref = f32[16,16,128]{2,1,0:T(8,128)S(1)} async-done(((f32[16,16,128]{2,1,0:T(8,128)}), f32[16,16,128]{2,1,0:T(8,128)S(1)}, u32[]{:S(2)}, u32[]{:S(2)}) %all-to-all-start.6) | async-done | bytes 131104 | tf_op jit(solution)/shard_map/all_to_all | solution.py:21
  119.9 0.9 normalize.1
  120.7 15.2 %all_to_all.45.in_ref = f32[16,24,128]{2,1,0:T(8,128)S(1)} all-to-all(f32[16,24,128]{2,1,0:T(8,128)S(1)} %get-tuple-element.37), channel_id=1, replica_groups=mesh['x'=4,'yh'=2,'core'=2,'ym'=2,'yl'=2,'zh'=4,'zl'=2] {'yh','ym','zh'}, dimensions={0} | all-to-all | bytes 393216 | tf_op jit(solution)/shard_map/all_to_all | solution.py:21
  135.9 6.1 %all-gather.1 = f32[48,128]{1,0:T(8,128)S(1)} all-gather(f32[24,128]{1,0:T(8,128)S(1)} %relay.1), channel_id=3, replica_groups=mesh['x'=4,'yh'=2,'core'=2,'ym'=2,'yl'=2,'zh'=4,'zl'=2] {'core'}, dimensions={0}, use_global_device_ids=true | all-gather | bytes 36864 | tf_op jit(solution)/shard_map/all_gather | solution.py:362
  142.0 2.8 %orthonormalize.1 = f32[32,64]{1,0:T(8,128)} custom-call(f32[2,24,128]{2,1,0:T(8,128)S(1)} %bitcast.2, f32[16,128]{1,0:T(8,128)S(1)} %get-tuple-element.38.update_ref), custom_call_target="tpu_custom_call" | custom-call | tf_op jit(solution)/shard_map/orthonormalize/pallas_call | solution.py:29
  (5 shorter events, 0.1 us)
Async XLA Ops:
  0.6 0.7 copy-start
  1.4 14.4 %copy-start.1 = (f32[32,64]{1,0:T(8,128)S(1)}, f32[32,64]{1,0:T(8,128)}, u32[]{:S(2)}) copy-start(f32[32,64]{1,0:T(8,128)} %basis_ref.1) | copy-start | bytes 24580
  16.5 25.7 %all-to-all-start.1 = ((bf16[16,32,256]{2,1,0:T(8,128)(2,1)}), bf16[16,32,256]{2,1,0:T(8,128)(2,1)S(1)}, u32[]{:S(2)}, u32[]{:S(2)}) async-start(bf16[16,32,256]{2,1,0:T(8,128)(2,1)} %get-tuple-element.21), calls=%async_computation.1 | async-start | bytes 524288 | tf_op jit(solution)/shard_map/all_to_all | solution.py:21
  30.3 12.8 %collective-permute-start = (bf16[16,32,256]{2,1,0:T(8,128)(2,1)S(1)}, bf16[16,32,256]{2,1,0:T(8,128)(2,1)S(1)}, u32[]{:S(2)}, u32[]{:S(2)}) collective-permute-start(bf16[16,32,256]{2,1,0:T(8,128)(2,1)S(1)} %all_to_all.40.after_ref.near_ref), channel_id=1, source_target_pairs={{0,32},{32,0},{1,33},{33,1},{2,34},{34,2},{3,35},{35,3},{4,36},{36... | collective-permute-start | bytes 786440 | tf_op jit(solution)/shard_map/ppermute | solution.py:25
  91.5 7.7 %collective-permute-start.1 = (f32[280,128]{1,0:T(8,128)S(1)}, f32[280,128]{1,0:T(8,128)S(1)}, u32[]{:S(2)}, u32[]{:S(2)}) collective-permute-start(f32[280,128]{1,0:T(8,128)S(1)} %get-tuple-element.33.sent_ref), channel_id=1, source_target_pairs={{0,32},{32,0},{1,33},{33,1},{2,34},{34,2},{3,35},{35,3},{4,36},{36... | collective-permute-start | bytes 430088 | tf_op jit(solution)/shard_map/ppermute | solution.py:25
  109.8 10.0 %all-to-all-start.6 = ((f32[16,16,128]{2,1,0:T(8,128)}), f32[16,16,128]{2,1,0:T(8,128)S(1)}, u32[]{:S(2)}, u32[]{:S(2)}) async-start(f32[16,16,128]{2,1,0:T(8,128)} %get-tuple-element.35), calls=%async_computation.6 | async-start | bytes 262144 | tf_op jit(solution)/shard_map/all_to_all | solution.py:21

commit v4 on v3

v4 whole, which is shorter than its diff:
```python
import math

import jax
import jax.numpy as jnp
from jax import lax
from jax.experimental import pallas as pl
from jax.experimental.pallas import tpu as pltpu
from jax.sharding import Mesh, PartitionSpec as P

AXES = ("x", "yh", "core", "ym", "yl", "zh", "zl")
SIZES = (4, 2, 2, 2, 2, 4, 2)
NEAR = ("x", "yl", "zl")
FAR = ("yh", "ym", "zh")
NN, NF = 16, 16
OWN, HALF, LINE = 32, 16, 256
HIGH = lax.Precision.HIGHEST
F32, BF16 = jnp.float32, jnp.bfloat16
VMEM = pl.BlockSpec(memory_space=pltpu.VMEM)
ANY = pl.BlockSpec(memory_space=pl.ANY)


def exchange(chunks, axes):
    return lax.all_to_all(chunks, axes, 0, 0, tiled=True)


def swap(value):
    return lax.ppermute(value, "core", [(0, 1), (1, 0)])


def call(body, outs, *args, specs=None, scratch=(), name=None):
    return pl.pallas_call(
        body,
        out_shape=outs,
        in_specs=specs or [VMEM] * len(args),
        out_specs=[VMEM] * len(outs),
        scratch_shapes=list(scratch),
        compiler_params=pltpu.CompilerParams(vmem_limit_bytes=48 * 1024 * 1024),
        name=name,
    )(*args)


def fold(block):
    half = block.shape[0] // 2
    return jnp.concatenate([block[:half], block[half:]], axis=1)


def unfold(packed):
    return jnp.concatenate([packed[:, :64], packed[:, 64:]], axis=0)


def total(ref):
    value = ref[0]
    for i in range(1, ref.shape[0]):
        value = value + ref[i]
    return value


def split(value):
    high = value.astype(BF16)
    rest = value - high.astype(F32)
    middle = rest.astype(BF16)
    return high, middle, (rest - middle.astype(F32)).astype(BF16)


def turn_out(packed):
    turned = jnp.transpose(packed)
    return jnp.concatenate([turned[:64], turned[64:]], axis=1)


def product(scaled, weights, axis):
    high, middle, low = (ref[...] for ref in weights)
    over = lambda left, right: lax.dot_general(
        left, right, (((1,), (axis,)), ((), ())), preferred_element_type=F32
    )
    top = over(scaled, high)
    part = over(scaled[:128], middle)
    return top[:64] + (top[64:128] + part[:64]) + (top[128:] + part[64:] + over(scaled[:64], low))


def turn_in(part):
    return jnp.transpose(jnp.concatenate([part[:, :LINE], part[:, LINE:]], axis=0))


def gram_of(packed):
    both = lax.dot_general(packed, packed, (((0,), (0,)), ((), ())), precision=HIGH, preferred_element_type=F32)
    return both[:64, :64] + both[64:, 64:]


def shrink(gram):
    blocks = gram[:32, :32], gram[32:, :32], gram[32:, 32:]
    rows = [jnp.concatenate([block[8 * j : 8 * j + 8] for j in range(4)], axis=1) for block in blocks]
    return jnp.concatenate(rows, axis=0)


def grow(packed):
    blocks = [
        jnp.concatenate([packed[8 * i : 8 * i + 8, 32 * j : 32 * j + 32] for j in range(4)], axis=0) for i in range(3)
    ]
    lower = jnp.concatenate(
        [
            jnp.concatenate([blocks[0], jnp.zeros((32, 32), F32)], axis=1),
            jnp.concatenate([blocks[1], blocks[2]], axis=1),
        ],
        axis=0,
    )
    return jnp.where(lax.broadcasted_iota(jnp.int32, (64, 64), 1) < 32, lower, jnp.transpose(lower))


def inverse_cholesky(gram):
    n = gram.shape[0]
    tiles = []
    sub = lax.broadcasted_iota(jnp.int32, (8, 128), 0)
    lane = lax.broadcasted_iota(jnp.int32, (8, 128), 1)
    for t in range(n // 8):
        eye = jnp.where(lane == sub + 8 * t + n, 1.0, 0.0).astype(F32)
        left = jnp.concatenate([gram[8 * t : 8 * t + 8], jnp.zeros((8, n), F32)], axis=1)
        tiles.append(left + eye)
    scale = [jnp.ones((8, 128), F32) for _ in tiles]
    for top in range(n // 8):
        cols = [
            {t: jnp.broadcast_to(tiles[t][:, 8 * top + j : 8 * top + j + 1], (8, 128)) for t in range(top, n // 8)}
            for j in range(8)
        ]
        for r in range(8):
            pivot = jnp.broadcast_to(cols[r][top][r : r + 1], (8, 128))
            scale[top] = jnp.where(sub == r, lax.rsqrt(pivot), scale[top])
            inv = 1.0 / pivot
            row = jnp.broadcast_to(tiles[top][r : r + 1], (8, 128))
            heads = [jnp.broadcast_to(cols[i][top][r : r + 1], (8, 128)) for i in range(r + 1, 8)]
            for t in range(top, n // 8):
                factor = cols[r][t] * inv
                if t == top:
                    factor = jnp.where(sub > r, factor, 0.0)
                tiles[t] = tiles[t] - factor * row
                for i in range(r + 1, 8):
                    cols[i][t] = cols[i][t] - factor * heads[i - r - 1]
    out = jnp.concatenate([tile * s for tile, s in zip(tiles, scale)], axis=0)
    return out[:, n:]


def rider_of(dinv):
    lane = lax.broadcasted_iota(jnp.int32, (8, 128), 1)
    return jnp.where(lane % 64 < 32, dinv[:8], dinv[8:])


def dinv_of(rider):
    low = lax.broadcasted_iota(jnp.int32, (8, 128), 1) % 64 < 32
    top = jnp.where(low, rider, pltpu.roll(rider, 32, 1))
    return jnp.concatenate([top, jnp.where(low, pltpu.roll(rider, 96, 1), rider)], axis=0)


def near_kernel(points_ref, out_ref):
    points = points_ref[...]
    for i in range(NN):
        out_ref[i] = points


def far_kernel(points_ref, basis_ref, after_ref, out_ref, fold_ref):
    points = points_ref[...]
    for i in range(NF):
        out_ref[i] = points
    fold_ref[...] = fold(basis_ref[...])


def affinity(near_ref, far_ref, out_refs):
    rows, cols = (
        jnp.concatenate([ref[i, h : h + HALF] for h in (0, HALF) for i in range(ref.shape[0])], axis=0)
        for ref in (near_ref, far_ref)
    )
    count, width = cols.shape
    rate = math.log2(math.e) / (0.25 * width)
    dots = lax.dot_general(rows, cols, (((1,), (1,)), ((), ())), preferred_element_type=F32)
    rows32, cols32 = rows.astype(F32), cols.astype(F32)
    rows_sq = jnp.sum(rows32 * rows32, axis=1, keepdims=True) * rate
    cols_sq = jnp.sum(cols32 * cols32, axis=1, keepdims=True) * rate
    cols_sq = jnp.transpose(jnp.broadcast_to(cols_sq, (count, 128)))[:1]
    weights = jnp.exp2(dots * (2.0 * rate) - (rows_sq + cols_sq))
    for ref, value in zip(out_refs, split(weights)):
        ref[...] = value
    sums = jnp.sum(weights, axis=0, keepdims=True)
    return jnp.concatenate([sums[:, 128 * i : 128 * i + 128] for i in range(count // 128)], axis=0)


def own_weights_kernel(near_ref, far_ref, high_ref, middle_ref, low_ref, sums_ref):
    sums_ref[:4] = affinity(near_ref, far_ref, (high_ref, middle_ref, low_ref))
    sums_ref[4:] = jnp.zeros((4, 128), F32)


def other_weights_kernel(near_ref, far_ref, sums_ref, basis_ref, high_ref, middle_ref, low_ref, out_ref):
    sums = affinity(near_ref, far_ref, (high_ref, middle_ref, low_ref))
    sums = sums_ref[...] + jnp.concatenate([sums, jnp.zeros((4, 128), F32)], axis=0)
    payload = jnp.concatenate([sums, basis_ref[...]], axis=0)
    for i in range(NF):
        out_ref[i] = payload


def first_kernel(*refs):
    own_refs, other_refs = refs[:3], refs[3:6]
    in_ref, part_ref, dinv_ref, deg_ref, dinvs_ref = refs[6:]
    head = in_ref[0, :8]
    for i in range(1, NF):
        head = head + in_ref[i, :8]
    mine = lax.axis_index(FAR)
    sub = lax.broadcasted_iota(jnp.int32, (8, 128), 0)
    lane = lax.broadcasted_iota(jnp.int32, (8, 128), 1)
    lines = []
    for h in range(2):
        line = jnp.sum(jnp.where(sub == 2 * h + mine // 8, head, 0.0), axis=0, keepdims=True)
        lines.append(pltpu.roll(jnp.broadcast_to(line, (8, 128)), (128 + HALF * h - HALF * (mine % 8)) % 128, 1))
    deg_ref[...] = jnp.where(lane < HALF, lines[0], lines[1])[0, :OWN]
    turned = jnp.transpose(lax.rsqrt(head))
    columns = [
        jnp.broadcast_to(jnp.concatenate([turned[:, 2 * h + i : 2 * h + i + 1] for i in range(2)], axis=0), (LINE, 128))
        for h in range(2)
    ]
    dinv = jnp.where(lax.broadcasted_iota(jnp.int32, (LINE, 128), 1) < 64, columns[0], columns[1])
    dinvs_ref[...] = dinv
    dinv_ref[...] = dinvs_ref[pl.ds(pl.multiple_of(mine * HALF, HALF), HALF)]
    packed = jnp.concatenate([in_ref[i, 8:] for i in range(NF)], axis=0)
    scaled = jnp.concatenate(split(turn_out(packed * dinv)), axis=0)
    for side, weights in enumerate((own_refs, other_refs)):
        part = turn_in(product(scaled, weights, 1))
        for i in range(NN):
            part_ref[i, HALF * side : HALF * side + HALF] = part[HALF * i : HALF * i + HALF]


def half_kernel(in_ref, dinv_ref, out_ref):
    out_ref[: 2 * HALF] = total(in_ref)
    out_ref[2 * HALF :] = dinv_ref[...]


def update_kernel(in_ref, out_ref):
    core = lax.axis_index("core")
    mine, other = in_ref[core], in_ref[1 - core]
    own_dinv, other_dinv = mine[2 * HALF :], other[2 * HALF :]
    payload = jnp.concatenate(
        [
            (mine[:HALF] + other[HALF : 2 * HALF]) * own_dinv,
            (mine[HALF : 2 * HALF] + other[:HALF]) * other_dinv,
            rider_of(own_dinv),
            rider_of(other_dinv),
        ],
        axis=0,
    )
    for i in range(NN):
        out_ref[i] = payload


def second_kernel(*refs):
    sides = refs[:3], refs[3:6]
    in_ref, out_ref, gram_ref = refs[6:]
    grams, parts = [], []
    for side, weights in enumerate(sides):
        updates, scaled = [], []
        for i in range(NN):
            update = in_ref[i, HALF * side : HALF * side + HALF]
            rider = in_ref[i, 2 * HALF + 8 * side : 2 * HALF + 8 * side + 8]
            updates.append(update)
            scaled.append(update * dinv_of(rider))
        scaled = jnp.concatenate(split(turn_out(jnp.concatenate(scaled, axis=0))), axis=0)
        parts.append(product(scaled, weights, 0))
        grams.append(gram_of(jnp.concatenate(updates, axis=0)))
    gram_ref[...] = shrink(grams[0] + grams[1])
    gram = gram_ref[pl.ds(pl.multiple_of(lax.axis_index("core") * 8, 8), 16)]
    part = turn_in(parts[0] + parts[1])
    for i in range(NF):
        out_ref[i, :HALF] = part[HALF * i : HALF * i + HALF]
        out_ref[i, HALF:] = gram


def collect_kernel(in_ref, dinv_ref, out_ref, gram_ref):
    value = total(in_ref)
    update = value[:HALF] * dinv_ref[...]
    gram_ref[...] = value[HALF:]
    for i in range(NF):
        out_ref[i] = update


def factor_kernel(gram_ref, inverse_ref):
    gram = jnp.concatenate([gram_ref[0], gram_ref[1, 8:]], axis=0)
    turned = jnp.transpose(inverse_cholesky(grow(gram)))
    none = jnp.zeros_like(turned)
    inverse_ref[:64] = jnp.concatenate([turned, none], axis=1)
    inverse_ref[64:] = jnp.concatenate([none, turned], axis=1)


def normalize_kernel(in_ref, inverse_ref, update_ref, out_ref, updates_ref):
    update = jnp.concatenate([in_ref[i] for i in range(NF)], axis=0)
    update = jnp.dot(update, inverse_ref[...], precision=HIGH, preferred_element_type=F32)
    updates_ref[...] = update
    mine = lax.axis_index(FAR)
    update_ref[...] = updates_ref[pl.ds(pl.multiple_of(mine * HALF, HALF), HALF)]
    gram = shrink(gram_of(update))
    for i in range(NN):
        out_ref[i] = gram


def relay_kernel(in_ref, out_ref):
    out_ref[...] = total(in_ref)


def final_kernel(in_ref, update_ref, out_ref):
    inverse = inverse_cholesky(grow(total(in_ref)))
    out_ref[...] = lax.dot_general(
        unfold(update_ref[...]), inverse, (((1,), (1,)), ((), ())), precision=HIGH, preferred_element_type=F32
    )


def per_device(points, basis):
    own, width = points.shape
    shape = lambda *dims, dtype=F32: jax.ShapeDtypeStruct(dims, dtype)
    (near,) = call(near_kernel, [shape(NN, own, width, dtype=BF16)], points, name="near_copies")
    near = exchange(near, NEAR)
    other = swap(near)
    far, basis = call(
        far_kernel,
        [shape(NF, own, width, dtype=BF16), shape(HALF, 128)],
        points,
        basis,
        near,
        specs=[VMEM, VMEM, ANY],
        name="far_copies",
    )
    far = exchange(far, FAR)
    parts = [shape(NN * own, NF * own, dtype=BF16)] * 3
    *own_weights, sums = call(own_weights_kernel, parts + [shape(8, 128)], near, far, name="own_weights")
    *other_weights, sums = call(
        other_weights_kernel, parts + [shape(NF, 8 + HALF, 128)], other, far, sums, basis, name="other_weights"
    )
    weights = own_weights + other_weights
    part, dinv, degree = call(
        first_kernel,
        [shape(NN, 2 * HALF, 128), shape(HALF, 128), shape(own)],
        *weights,
        exchange(sums, FAR),
        scratch=[pltpu.VMEM((LINE, 128), F32)],
        name="first_product",
    )
    (part,) = call(half_kernel, [shape(3 * HALF, 128)], exchange(part, NEAR), dinv, name="half_update")
    (update,) = call(update_kernel, [shape(NN, 2 * HALF + 16, 128)], lax.all_gather(part, "core"), name="first_update")
    (part,) = call(
        second_kernel,
        [shape(NF, HALF + 16, 128)],
        *weights,
        exchange(update, NEAR),
        scratch=[pltpu.VMEM((24, 128), F32)],
        name="second_product",
    )
    update, gram = call(
        collect_kernel, [shape(NF, HALF, 128), shape(16, 128)], exchange(part, FAR), dinv, name="collect"
    )
    everyone = exchange(update, FAR)
    (inverse,) = call(factor_kernel, [shape(128, 128)], lax.all_gather(gram, "core"), name="factor")
    update, gram = call(
        normalize_kernel,
        [shape(HALF, 128), shape(NN, 24, 128)],
        everyone,
        inverse,
        scratch=[pltpu.VMEM((LINE, 128), F32)],
        name="normalize",
    )
    (gram,) = call(relay_kernel, [shape(24, 128)], exchange(gram, NEAR), name="relay")
    (out,) = call(final_kernel, [shape(own, 64)], lax.all_gather(gram, "core"), update, name="orthonormalize")
    return (out, degree)


def solution(mesh):
    fine = Mesh(mesh.devices.reshape(SIZES), AXES)
    return jax.shard_map(
        per_device,
        mesh=fine,
        in_specs=(P(AXES, None), P(AXES, None)),
        out_specs=(P(AXES, None), P(AXES)),
        check_vma=False,
    )
```

time: 145 us -> 144 us (level)
  starting transfers between devices: 28.2 us -> 23.7 us
  blocking collectives: 90.6 us -> 93.2 us
    ppermute x2 -> x1, starting transfers between devices: 10.7 us -> 4.02 us  [swap(): return lax.ppermute(value, 'core', [(0, 1), (1, 0)])]
    all_gather x1 -> x2, blocking collectives: 6.05 us -> 9.66 us  [per_device(): lax.all_gather(gram, 'core')]
    all_to_all x6, blocking collectives: 79.5 us -> 77.4 us  [exchange(): return lax.all_to_all(chunks, axes, 0, 0, tiled=True)]
    all_to_all x2, starting transfers between devices: 17.5 us -> 19.6 us  [exchange(): return lax.all_to_all(chunks, axes, 0, 0, tiled=True)]
    pallas_call x15 -> x13, Pallas kernels: 12 us -> 11.9 us  [call(): pl.pallas_call(body, out_shape=outs, in_specs=specs or [VMEM] * len(args)...]
  transfers between devices with their start and end apart: 4 -> 3, of which waited for: 3 -> 2; matrix products, arithmetic and copies ran while one was open for 0% -> 0% of each run, Pallas kernels for 2% -> 2%
where the time goes in v4:
time: 144 us; the launch traced here: 143 us
  blocking collectives  93.2 us (65%)
  starting transfers between devices  23.7 us (16%)
  waiting for transfers between devices  13.2 us (9%)
  Pallas kernels  11.9 us (8%)
    all_to_all x6, blocking collectives, exchange(): return lax.all_to_all(chunks, axes, 0, 0, tiled=True)  77.4 us
    all_to_all x2, starting transfers between devices, exchange(): return lax.all_to_all(chunks, axes, 0, 0, tiled=True)  19.6 us
    all_to_all x2, waiting for transfers between devices, exchange(): return lax.all_to_all(chunks, axes, 0, 0, tiled=True)  13.2 us
    pallas_call x13, Pallas kernels, call(): pl.pallas_call(body, out_shape=outs, in_specs=specs or [VMEM] * len(args)...  11.9 us
    all_gather x2, blocking collectives, per_device(): lax.all_gather(gram, 'core')  9.66 us
    all_gather x1, blocking collectives, per_device(): lax.all_gather(part, 'core')  6.16 us
    ppermute x1, starting transfers between devices, swap(): return lax.ppermute(value, 'core', [(0, 1), (1, 0)])  4.02 us
  transfers between devices with their start and end apart: 3, of which 2 were waited for; matrix products, arithmetic and copies ran while one was open for 0% of the time, Pallas kernels for 2%

profile of v4, /device:TPU:1, one launch (start us, length us, event | category | flops | bytes accessed | tf_op | source)
XLA Modules:
  0.0 143.4 jit_solution(2468137827879686515)
XLA Ops:
  0.6 0.0 copy-start
  0.6 0.7 copy-done
  1.4 0.0 copy-start.1
  1.4 14.4 %all_to_all.40.after_ref.near_ref = bf16[16,32,256]{2,1,0:T(8,128)(2,1)S(1)} all-to-all(bf16[16,32,256]{2,1,0:T(8,128)(2,1)S(1)} %near_copies.1), channel_id=1, replica_groups=mesh['x'=4,'yh'=2,'core'=2,'ym'=2,'yl'=2,'zh'=4,'zl'=2] {'x','yl','zl'}, dimensions={0} | all-to-all | bytes 524288 | tf_op jit(solution)/shard_map/all_to_all | solution.py:23
  15.8 0.0 copy-done.1
  15.8 0.7 far_copies.1
  16.5 13.8 %all-to-all-start.1 = ((bf16[16,32,256]{2,1,0:T(8,128)(2,1)}), bf16[16,32,256]{2,1,0:T(8,128)(2,1)S(1)}, u32[]{:S(2)}, u32[]{:S(2)}) async-start(bf16[16,32,256]{2,1,0:T(8,128)(2,1)} %get-tuple-element.19), calls=%async_computation.1 | async-start | bytes 524288 | tf_op jit(solution)/shard_map/all_to_all | solution.py:23
  30.3 4.0 %collective-permute-start = (bf16[16,32,256]{2,1,0:T(8,128)(2,1)S(1)}, bf16[16,32,256]{2,1,0:T(8,128)(2,1)S(1)}, u32[]{:S(2)}, u32[]{:S(2)}) collective-permute-start(bf16[16,32,256]{2,1,0:T(8,128)(2,1)S(1)} %all_to_all.40.after_ref.near_ref), channel_id=1, source_target_pairs={{0,32},{32,0},{1,33},{33,1},{2,34},{34,2},{3,35},{35,3},{4,36},{36... | collective-permute-start | bytes 786440 | tf_op jit(solution)/shard_map/ppermute | solution.py:27
  34.3 7.9 %all-to-all-done.1.far_ref = bf16[16,32,256]{2,1,0:T(8,128)(2,1)S(1)} async-done(((bf16[16,32,256]{2,1,0:T(8,128)(2,1)}), bf16[16,32,256]{2,1,0:T(8,128)(2,1)S(1)}, u32[]{:S(2)}, u32[]{:S(2)}) %all-to-all-start.1) | async-done | bytes 262176 | tf_op jit(solution)/shard_map/all_to_all | solution.py:23
  42.2 0.8 own_weights.1
  43.0 0.0 collective-permute-done.near_ref
  43.0 0.8 other_weights.1
  43.8 16.2 %all_to_all.41.refs_6_ = f32[16,24,128]{2,1,0:T(8,128)S(1)} all-to-all(f32[16,24,128]{2,1,0:T(8,128)S(1)} %get-tuple-element.28), channel_id=1, replica_groups=mesh['x'=4,'yh'=2,'core'=2,'ym'=2,'yl'=2,'zh'=4,'zl'=2] {'yh','ym','zh'}, dimensions={0} | all-to-all | bytes 393216 | tf_op jit(solution)/shard_map/all_to_all | solution.py:23
  60.1 1.8 %first_product.1 = (f32[16,32,128]{2,1,0:T(8,128)S(1)}, f32[16,128]{1,0:T(8,128)S(1)}, f32[32]{0:T(128)}) custom-call(bf16[512,512]{1,0:T(8,128)(2,1)S(1)} %get-tuple-element.20.refs_0_, bf16[512,512]{1,0:T(8,128)(2,1)S(1)} %get-tuple-element.21.refs_1_, bf16[512,512]{1,0:T(8,128)(2,1)S(1)} %get-tuple-element.22.refs_2_, ...), custom_call_target="tpu_custom_call" | custom-call | tf_op jit(solution)/shard_map/first_product/pallas_call | solution.py:31
  61.9 10.5 %all_to_all.42.in_ref = f32[16,32,128]{2,1,0:T(8,128)S(1)} all-to-all(f32[16,32,128]{2,1,0:T(8,128)S(1)} %get-tuple-element.29), channel_id=1, replica_groups=mesh['x'=4,'yh'=2,'core'=2,'ym'=2,'yl'=2,'zh'=4,'zl'=2] {'x','yl','zl'}, dimensions={0} | all-to-all | bytes 524288 | tf_op jit(solution)/shard_map/all_to_all | solution.py:23
  72.4 6.2 %all-gather = f32[96,128]{1,0:T(8,128)S(1)} all-gather(f32[48,128]{1,0:T(8,128)S(1)} %half_update.1), channel_id=2, replica_groups=mesh['x'=4,'yh'=2,'core'=2,'ym'=2,'yl'=2,'zh'=4,'zl'=2] {'core'}, dimensions={0}, use_global_device_ids=true | all-gather | bytes 73728 | tf_op jit(solution)/shard_map/all_gather | solution.py:340
  78.6 10.5 %all_to_all.43.refs_6_ = f32[16,48,128]{2,1,0:T(8,128)S(1)} all-to-all(f32[16,48,128]{2,1,0:T(8,128)S(1)} %first_update.1), channel_id=1, replica_groups=mesh['x'=4,'yh'=2,'core'=2,'ym'=2,'yl'=2,'zh'=4,'zl'=2] {'x','yl','zl'}, dimensions={0} | all-to-all | bytes 786432 | tf_op jit(solution)/shard_map/all_to_all | solution.py:23
  89.1 1.2 second_product.1
  90.3 15.3 %all_to_all.44.in_ref = f32[16,32,128]{2,1,0:T(8,128)S(1)} all-to-all(f32[16,32,128]{2,1,0:T(8,128)S(1)} %second_product.1), channel_id=1, replica_groups=mesh['x'=4,'yh'=2,'core'=2,'ym'=2,'yl'=2,'zh'=4,'zl'=2] {'yh','ym','zh'}, dimensions={0} | all-to-all | bytes 524288 | tf_op jit(solution)/shard_map/all_to_all | solution.py:23
  105.6 0.7 collect.1
  106.3 5.9 %all-to-all-start.6 = ((f32[16,16,128]{2,1,0:T(8,128)}), f32[16,16,128]{2,1,0:T(8,128)S(1)}, u32[]{:S(2)}, u32[]{:S(2)}) async-start(f32[16,16,128]{2,1,0:T(8,128)} %get-tuple-element.31), calls=%async_computation.6 | async-start | bytes 262144 | tf_op jit(solution)/shard_map/all_to_all | solution.py:23
  112.2 4.1 %all-gather.1 = f32[32,128]{1,0:T(8,128)S(1)} all-gather(f32[16,128]{1,0:T(8,128)S(1)} %get-tuple-element.32), channel_id=3, replica_groups=mesh['x'=4,'yh'=2,'core'=2,'ym'=2,'yl'=2,'zh'=4,'zl'=2] {'core'}, dimensions={0}, use_global_device_ids=true | all-gather | bytes 24576 | tf_op jit(solution)/shard_map/all_gather | solution.py:353
  116.3 2.1 %factor.1.inverse_ref = f32[128,128]{1,0:T(8,128)S(1)} custom-call(f32[2,16,128]{2,1,0:T(8,128)S(1)} %bitcast.5), custom_call_target="tpu_custom_call" | custom-call | tf_op jit(solution)/shard_map/factor/pallas_call | solution.py:31
  118.5 5.3 %all-to-all-done.6.in_ref = f32[16,16,128]{2,1,0:T(8,128)S(1)} async-done(((f32[16,16,128]{2,1,0:T(8,128)}), f32[16,16,128]{2,1,0:T(8,128)S(1)}, u32[]{:S(2)}, u32[]{:S(2)}) %all-to-all-start.6) | async-done | bytes 131104 | tf_op jit(solution)/shard_map/all_to_all | solution.py:23
  123.8 0.9 normalize.1
  124.6 10.4 %all_to_all.45.in_ref = f32[16,24,128]{2,1,0:T(8,128)S(1)} all-to-all(f32[16,24,128]{2,1,0:T(8,128)S(1)} %get-tuple-element.33), channel_id=1, replica_groups=mesh['x'=4,'yh'=2,'core'=2,'ym'=2,'yl'=2,'zh'=4,'zl'=2] {'x','yl','zl'}, dimensions={0} | all-to-all | bytes 393216 | tf_op jit(solution)/shard_map/all_to_all | solution.py:23
  135.1 5.5 %all-gather.2 = f32[48,128]{1,0:T(8,128)S(1)} all-gather(f32[24,128]{1,0:T(8,128)S(1)} %relay.1), channel_id=4, replica_groups=mesh['x'=4,'yh'=2,'core'=2,'ym'=2,'yl'=2,'zh'=4,'zl'=2] {'core'}, dimensions={0}, use_global_device_ids=true | all-gather | bytes 36864 | tf_op jit(solution)/shard_map/all_gather | solution.py:363
  140.6 2.8 %orthonormalize.1 = f32[32,64]{1,0:T(8,128)} custom-call(f32[2,24,128]{2,1,0:T(8,128)S(1)} %bitcast.4, f32[16,128]{1,0:T(8,128)S(1)} %get-tuple-element.34.update_ref), custom_call_target="tpu_custom_call" | custom-call | tf_op jit(solution)/shard_map/orthonormalize/pallas_call | solution.py:31
  (4 shorter events, 0.1 us)
Async XLA Ops:
  0.6 0.7 copy-start
  1.4 14.4 %copy-start.1 = (f32[32,64]{1,0:T(8,128)S(1)}, f32[32,64]{1,0:T(8,128)}, u32[]{:S(2)}) copy-start(f32[32,64]{1,0:T(8,128)} %basis_ref.1) | copy-start | bytes 24580
  16.5 25.7 %all-to-all-start.1 = ((bf16[16,32,256]{2,1,0:T(8,128)(2,1)}), bf16[16,32,256]{2,1,0:T(8,128)(2,1)S(1)}, u32[]{:S(2)}, u32[]{:S(2)}) async-start(bf16[16,32,256]{2,1,0:T(8,128)(2,1)} %get-tuple-element.19), calls=%async_computation.1 | async-start | bytes 524288 | tf_op jit(solution)/shard_map/all_to_all | solution.py:23
  30.3 12.8 %collective-permute-start = (bf16[16,32,256]{2,1,0:T(8,128)(2,1)S(1)}, bf16[16,32,256]{2,1,0:T(8,128)(2,1)S(1)}, u32[]{:S(2)}, u32[]{:S(2)}) collective-permute-start(bf16[16,32,256]{2,1,0:T(8,128)(2,1)S(1)} %all_to_all.40.after_ref.near_ref), channel_id=1, source_target_pairs={{0,32},{32,0},{1,33},{33,1},{2,34},{34,2},{3,35},{35,3},{4,36},{36... | collective-permute-start | bytes 786440 | tf_op jit(solution)/shard_map/ppermute | solution.py:27
  106.3 17.5 %all-to-all-start.6 = ((f32[16,16,128]{2,1,0:T(8,128)}), f32[16,16,128]{2,1,0:T(8,128)S(1)}, u32[]{:S(2)}, u32[]{:S(2)}) async-start(f32[16,16,128]{2,1,0:T(8,128)} %get-tuple-element.31), calls=%async_computation.6 | async-start | bytes 262144 | tf_op jit(solution)/shard_map/all_to_all | solution.py:23

commit v5 on v4

--- a/solution.py
+++ b/solution.py
@@ -68,13 +68,13 @@
 
 
 def product(scaled, weights, axis):
-    high, middle, low = (ref[...] for ref in weights)
+    high, middle = (ref[...] for ref in weights)
     over = lambda left, right: lax.dot_general(
         left, right, (((1,), (axis,)), ((), ())), preferred_element_type=F32
     )
     top = over(scaled, high)
     part = over(scaled[:128], middle)
-    return top[:64] + (top[64:128] + part[:64]) + (top[128:] + part[64:] + over(scaled[:64], low))
+    return top[:64] + (top[64:128] + part[:64]) + (top[128:] + part[64:])
 
 
 def turn_in(part):
@@ -162,41 +162,48 @@
     fold_ref[...] = fold(basis_ref[...])
 
 
-def affinity(near_ref, far_ref, out_refs):
-    rows, cols = (
-        jnp.concatenate([ref[i, h : h + HALF] for h in (0, HALF) for i in range(ref.shape[0])], axis=0)
-        for ref in (near_ref, far_ref)
-    )
+def line_of(ref):
+    return jnp.concatenate([ref[i, h : h + HALF] for h in (0, HALF) for i in range(ref.shape[0])], axis=0)
+
+
+def squares(points, rate):
+    floats = points.astype(F32)
+    return jnp.sum(floats * floats, axis=1, keepdims=True) * rate
+
+
+def rate_of(width):
+    return math.log2(math.e) / (0.25 * width)
+
+
+def line_kernel(near_ref, rows_ref, squares_ref):
+    rows = line_of(near_ref)
+    rows_ref[...] = rows
+    squares_ref[...] = jnp.broadcast_to(squares(rows, rate_of(rows.shape[1])), squares_ref.shape)
+
+
+def weights_kernel(own_ref, own_sq_ref, other_ref, other_sq_ref, far_ref, basis_ref, *refs):
+    cols = line_of(far_ref)
     count, width = cols.shape
-    rate = math.log2(math.e) / (0.25 * width)
-    dots = lax.dot_general(rows, cols, (((1,), (1,)), ((), ())), preferred_element_type=F32)
-    rows32, cols32 = rows.astype(F32), cols.astype(F32)
-    rows_sq = jnp.sum(rows32 * rows32, axis=1, keepdims=True) * rate
-    cols_sq = jnp.sum(cols32 * cols32, axis=1, keepdims=True) * rate
-    cols_sq = jnp.transpose(jnp.broadcast_to(cols_sq, (count, 128)))[:1]
-    weights = jnp.exp2(dots * (2.0 * rate) - (rows_sq + cols_sq))
-    for ref, value in zip(out_refs, split(weights)):
-        ref[...] = value
-    sums = jnp.sum(weights, axis=0, keepdims=True)
-    return jnp.concatenate([sums[:, 128 * i : 128 * i + 128] for i in range(count // 128)], axis=0)
-
-
-def own_weights_kernel(near_ref, far_ref, high_ref, middle_ref, low_ref, sums_ref):
-    sums_ref[:4] = affinity(near_ref, far_ref, (high_ref, middle_ref, low_ref))
-    sums_ref[4:] = jnp.zeros((4, 128), F32)
-
-
-def other_weights_kernel(near_ref, far_ref, sums_ref, basis_ref, high_ref, middle_ref, low_ref, out_ref):
-    sums = affinity(near_ref, far_ref, (high_ref, middle_ref, low_ref))
-    sums = sums_ref[...] + jnp.concatenate([sums, jnp.zeros((4, 128), F32)], axis=0)
-    payload = jnp.concatenate([sums, basis_ref[...]], axis=0)
+    rate = rate_of(width)
+    cols_sq = jnp.transpose(jnp.broadcast_to(squares(cols, rate), (count, 128)))[:1]
+    sums = []
+    for rows_ref, sq_ref, high_ref, middle_ref in ((own_ref, own_sq_ref, *refs[:2]), (other_ref, other_sq_ref, *refs[2:4])):
+        dots = lax.dot_general(rows_ref[...], cols, (((1,), (1,)), ((), ())), preferred_element_type=F32)
+        weights = jnp.exp2(dots * (2.0 * rate) - (jnp.tile(sq_ref[...], (1, count // 128)) + cols_sq))
+        high = weights.astype(BF16)
+        high_ref[...] = high
+        middle_ref[...] = (weights - high.astype(F32)).astype(BF16)
+        sums.append(jnp.sum(weights, axis=0, keepdims=True))
+    sums = sums[0] + sums[1]
+    lines = [sums[:, 128 * i : 128 * i + 128] for i in range(count // 128)]
+    payload = jnp.concatenate(lines + [jnp.zeros((4, 128), F32), basis_ref[...]], axis=0)
     for i in range(NF):
-        out_ref[i] = payload
+        refs[4][i] = payload
 
 
 def first_kernel(*refs):
-    own_refs, other_refs = refs[:3], refs[3:6]
-    in_ref, part_ref, dinv_ref, deg_ref, dinvs_ref = refs[6:]
+    own_refs, other_refs = refs[:2], refs[2:4]
+    in_ref, part_ref, dinv_ref, deg_ref, dinvs_ref = refs[4:]
     head = in_ref[0, :8]
     for i in range(1, NF):
         head = head + in_ref[i, :8]
@@ -247,8 +254,8 @@
 
 
 def second_kernel(*refs):
-    sides = refs[:3], refs[3:6]
-    in_ref, out_ref, gram_ref = refs[6:]
+    sides = refs[:2], refs[2:4]
+    in_ref, out_ref, gram_ref = refs[4:]
     grams, parts = [], []
     for side, weights in enumerate(sides):
         updates, scaled = [], []
@@ -322,12 +329,19 @@
         name="far_copies",
     )
     far = exchange(far, FAR)
-    parts = [shape(NN * own, NF * own, dtype=BF16)] * 3
-    *own_weights, sums = call(own_weights_kernel, parts + [shape(8, 128)], near, far, name="own_weights")
-    *other_weights, sums = call(
-        other_weights_kernel, parts + [shape(NF, 8 + HALF, 128)], other, far, sums, basis, name="other_weights"
-    )
-    weights = own_weights + other_weights
+    lines = []
+    for name, value in (("own", near), ("other", other)):
+        lines += call(
+            line_kernel, [shape(NN * own, width, dtype=BF16), shape(NN * own, 128)], value, name=name + "_line"
+        )
+    *weights, sums = call(
+        weights_kernel,
+        [shape(NN * own, NF * own, dtype=BF16)] * 4 + [shape(NF, 8 + HALF, 128)],
+        *lines,
+        far,
+        basis,
+        name="weights",
+    )
     part, dinv, degree = call(
         first_kernel,
         [shape(NN, 2 * HALF, 128), shape(HALF, 128), shape(own)],

time: 144 us -> 143 us (level)
    pallas_call x13 -> x14, Pallas kernels: 11.9 us -> 10.9 us  [call(): pl.pallas_call(body, out_shape=outs, in_specs=specs or [VMEM] * len(args)...]
  transfers between devices with their start and end apart: 3 -> 3, of which waited for: 2 -> 3; matrix products, arithmetic and copies ran while one was open for 0% -> 0% of each run, Pallas kernels for 2% -> 2%
where the time goes in v5:
time: 143 us; the launch traced here: 142 us
  blocking collectives  93.3 us (65%)
  starting transfers between devices  23.6 us (17%)
  waiting for transfers between devices  12.9 us (9%)
  Pallas kernels  10.9 us (8%)
    all_to_all x6, blocking collectives, exchange(): return lax.all_to_all(chunks, axes, 0, 0, tiled=True)  77.3 us
    all_to_all x2, starting transfers between devices, exchange(): return lax.all_to_all(chunks, axes, 0, 0, tiled=True)  19.6 us
    all_to_all x2, waiting for transfers between devices, exchange(): return lax.all_to_all(chunks, axes, 0, 0, tiled=True)  11.9 us
    pallas_call x14, Pallas kernels, call(): pl.pallas_call(body, out_shape=outs, in_specs=specs or [VMEM] * len(args)...  10.9 us
    all_gather x2, blocking collectives, per_device(): lax.all_gather(gram, 'core')  9.69 us
    all_gather x1, blocking collectives, per_device(): lax.all_gather(part, 'core')  6.23 us
    ppermute x1, starting transfers between devices, swap(): return lax.ppermute(value, 'core', [(0, 1), (1, 0)])  4.02 us
  transfers between devices with their start and end apart: 3, of which 3 were waited for; matrix products, arithmetic and copies ran while one was open for 0% of the time, Pallas kernels for 2%

profile of v5, /device:TPU:1, one launch (start us, length us, event | category | flops | bytes accessed | tf_op | source)
XLA Modules:
  0.0 142.1 jit_solution(353119916798754003)
XLA Ops:
  0.6 0.0 copy-start
  0.6 0.7 copy-done
  1.4 0.0 copy-start.1
  1.4 14.4 %all_to_all.40.near_ref.after_ref = bf16[16,32,256]{2,1,0:T(8,128)(2,1)S(1)} all-to-all(bf16[16,32,256]{2,1,0:T(8,128)(2,1)S(1)} %near_copies.1), channel_id=1, replica_groups=mesh['x'=4,'yh'=2,'core'=2,'ym'=2,'yl'=2,'zh'=4,'zl'=2] {'x','yl','zl'}, dimensions={0} | all-to-all | bytes 524288 | tf_op jit(solution)/shard_map/all_to_all | solution.py:23
  15.8 0.0 copy-done.1
  15.8 0.7 far_copies.1
  16.5 13.8 %all-to-all-start.1 = ((bf16[16,32,256]{2,1,0:T(8,128)(2,1)}), bf16[16,32,256]{2,1,0:T(8,128)(2,1)S(1)}, u32[]{:S(2)}, u32[]{:S(2)}) async-start(bf16[16,32,256]{2,1,0:T(8,128)(2,1)} %get-tuple-element.24), calls=%async_computation.1 | async-start | bytes 524288 | tf_op jit(solution)/shard_map/all_to_all | solution.py:23
  30.3 4.0 %collective-permute-start = (bf16[16,32,256]{2,1,0:T(8,128)(2,1)S(1)}, bf16[16,32,256]{2,1,0:T(8,128)(2,1)S(1)}, u32[]{:S(2)}, u32[]{:S(2)}) collective-permute-start(bf16[16,32,256]{2,1,0:T(8,128)(2,1)S(1)} %all_to_all.40.near_ref.after_ref), channel_id=1, source_target_pairs={{0,32},{32,0},{1,33},{33,1},{2,34},{34,2},{3,35},{35,3},{4,36},{36... | collective-permute-start | bytes 786440 | tf_op jit(solution)/shard_map/ppermute | solution.py:27
  34.3 0.1 own_line.1
  34.4 1.0 collective-permute-done.near_ref
  35.4 0.1 other_line.1
  35.6 6.6 %all-to-all-done.1.far_ref = bf16[16,32,256]{2,1,0:T(8,128)(2,1)S(1)} async-done(((bf16[16,32,256]{2,1,0:T(8,128)(2,1)}), bf16[16,32,256]{2,1,0:T(8,128)(2,1)S(1)}, u32[]{:S(2)}, u32[]{:S(2)}) %all-to-all-start.1) | async-done | bytes 262176 | tf_op jit(solution)/shard_map/all_to_all | solution.py:23
  42.2 0.8 weights.1
  43.0 16.5 %all_to_all.41.refs_4_ = f32[16,24,128]{2,1,0:T(8,128)S(1)} all-to-all(f32[16,24,128]{2,1,0:T(8,128)S(1)} %get-tuple-element.30), channel_id=1, replica_groups=mesh['x'=4,'yh'=2,'core'=2,'ym'=2,'yl'=2,'zh'=4,'zl'=2] {'yh','ym','zh'}, dimensions={0} | all-to-all | bytes 393216 | tf_op jit(solution)/shard_map/all_to_all | solution.py:23
  59.6 1.5 %first_product.1 = (f32[16,32,128]{2,1,0:T(8,128)S(1)}, f32[16,128]{1,0:T(8,128)S(1)}, f32[32]{0:T(128)}) custom-call(bf16[512,512]{1,0:T(8,128)(2,1)S(1)} %get-tuple-element.26.refs_0_, bf16[512,512]{1,0:T(8,128)(2,1)S(1)} %get-tuple-element.27.refs_1_, bf16[512,512]{1,0:T(8,128)(2,1)S(1)} %get-tuple-element.28.refs_2_, ...), custom_call_target="tpu_custom_call" | custom-call | tf_op jit(solution)/shard_map/first_product/pallas_call | solution.py:31
  61.1 10.2 %all_to_all.42.in_ref = f32[16,32,128]{2,1,0:T(8,128)S(1)} all-to-all(f32[16,32,128]{2,1,0:T(8,128)S(1)} %get-tuple-element.31), channel_id=1, replica_groups=mesh['x'=4,'yh'=2,'core'=2,'ym'=2,'yl'=2,'zh'=4,'zl'=2] {'x','yl','zl'}, dimensions={0} | all-to-all | bytes 524288 | tf_op jit(solution)/shard_map/all_to_all | solution.py:23
  71.3 6.2 %all-gather = f32[96,128]{1,0:T(8,128)S(1)} all-gather(f32[48,128]{1,0:T(8,128)S(1)} %half_update.1), channel_id=2, replica_groups=mesh['x'=4,'yh'=2,'core'=2,'ym'=2,'yl'=2,'zh'=4,'zl'=2] {'core'}, dimensions={0}, use_global_device_ids=true | all-gather | bytes 73728 | tf_op jit(solution)/shard_map/all_gather | solution.py:354
  77.6 10.5 %all_to_all.43.refs_4_ = f32[16,48,128]{2,1,0:T(8,128)S(1)} all-to-all(f32[16,48,128]{2,1,0:T(8,128)S(1)} %first_update.1), channel_id=1, replica_groups=mesh['x'=4,'yh'=2,'core'=2,'ym'=2,'yl'=2,'zh'=4,'zl'=2] {'x','yl','zl'}, dimensions={0} | all-to-all | bytes 786432 | tf_op jit(solution)/shard_map/all_to_all | solution.py:23
  88.1 1.0 second_product.1
  89.1 15.2 %all_to_all.44.in_ref = f32[16,32,128]{2,1,0:T(8,128)S(1)} all-to-all(f32[16,32,128]{2,1,0:T(8,128)S(1)} %second_product.1), channel_id=1, replica_groups=mesh['x'=4,'yh'=2,'core'=2,'ym'=2,'yl'=2,'zh'=4,'zl'=2] {'yh','ym','zh'}, dimensions={0} | all-to-all | bytes 524288 | tf_op jit(solution)/shard_map/all_to_all | solution.py:23
  104.4 0.7 collect.1
  105.0 5.9 %all-to-all-start.6 = ((f32[16,16,128]{2,1,0:T(8,128)}), f32[16,16,128]{2,1,0:T(8,128)S(1)}, u32[]{:S(2)}, u32[]{:S(2)}) async-start(f32[16,16,128]{2,1,0:T(8,128)} %get-tuple-element.33), calls=%async_computation.6 | async-start | bytes 262144 | tf_op jit(solution)/shard_map/all_to_all | solution.py:23
  110.9 4.1 %all-gather.1 = f32[32,128]{1,0:T(8,128)S(1)} all-gather(f32[16,128]{1,0:T(8,128)S(1)} %get-tuple-element.34), channel_id=3, replica_groups=mesh['x'=4,'yh'=2,'core'=2,'ym'=2,'yl'=2,'zh'=4,'zl'=2] {'core'}, dimensions={0}, use_global_device_ids=true | all-gather | bytes 24576 | tf_op jit(solution)/shard_map/all_gather | solution.py:367
  115.1 2.1 %factor.1.inverse_ref = f32[128,128]{1,0:T(8,128)S(1)} custom-call(f32[2,16,128]{2,1,0:T(8,128)S(1)} %bitcast.5), custom_call_target="tpu_custom_call" | custom-call | tf_op jit(solution)/shard_map/factor/pallas_call | solution.py:31
  117.2 5.3 %all-to-all-done.6.in_ref = f32[16,16,128]{2,1,0:T(8,128)S(1)} async-done(((f32[16,16,128]{2,1,0:T(8,128)}), f32[16,16,128]{2,1,0:T(8,128)S(1)}, u32[]{:S(2)}, u32[]{:S(2)}) %all-to-all-start.6) | async-done | bytes 131104 | tf_op jit(solution)/shard_map/all_to_all | solution.py:23
  122.5 0.9 normalize.1
  123.3 10.4 %all_to_all.45.in_ref = f32[16,24,128]{2,1,0:T(8,128)S(1)} all-to-all(f32[16,24,128]{2,1,0:T(8,128)S(1)} %get-tuple-element.35), channel_id=1, replica_groups=mesh['x'=4,'yh'=2,'core'=2,'ym'=2,'yl'=2,'zh'=4,'zl'=2] {'x','yl','zl'}, dimensions={0} | all-to-all | bytes 393216 | tf_op jit(solution)/shard_map/all_to_all | solution.py:23
  133.8 5.5 %all-gather.2 = f32[48,128]{1,0:T(8,128)S(1)} all-gather(f32[24,128]{1,0:T(8,128)S(1)} %relay.1), channel_id=4, replica_groups=mesh['x'=4,'yh'=2,'core'=2,'ym'=2,'yl'=2,'zh'=4,'zl'=2] {'core'}, dimensions={0}, use_global_device_ids=true | all-gather | bytes 36864 | tf_op jit(solution)/shard_map/all_gather | solution.py:377
  139.3 2.8 %orthonormalize.1 = f32[32,64]{1,0:T(8,128)} custom-call(f32[2,24,128]{2,1,0:T(8,128)S(1)} %bitcast.4, f32[16,128]{1,0:T(8,128)S(1)} %get-tuple-element.36.update_ref), custom_call_target="tpu_custom_call" | custom-call | tf_op jit(solution)/shard_map/orthonormalize/pallas_call | solution.py:31
  (4 shorter events, 0.1 us)
Async XLA Ops:
  0.6 0.7 copy-start
  1.4 14.4 %copy-start.1 = (f32[32,64]{1,0:T(8,128)S(1)}, f32[32,64]{1,0:T(8,128)}, u32[]{:S(2)}) copy-start(f32[32,64]{1,0:T(8,128)} %basis_ref.1) | copy-start | bytes 24580
  16.5 25.7 %all-to-all-start.1 = ((bf16[16,32,256]{2,1,0:T(8,128)(2,1)}), bf16[16,32,256]{2,1,0:T(8,128)(2,1)S(1)}, u32[]{:S(2)}, u32[]{:S(2)}) async-start(bf16[16,32,256]{2,1,0:T(8,128)(2,1)} %get-tuple-element.24), calls=%async_computation.1 | async-start | bytes 524288 | tf_op jit(solution)/shard_map/all_to_all | solution.py:23
  30.3 5.2 %collective-permute-start = (bf16[16,32,256]{2,1,0:T(8,128)(2,1)S(1)}, bf16[16,32,256]{2,1,0:T(8,128)(2,1)S(1)}, u32[]{:S(2)}, u32[]{:S(2)}) collective-permute-start(bf16[16,32,256]{2,1,0:T(8,128)(2,1)S(1)} %all_to_all.40.near_ref.after_ref), channel_id=1, source_target_pairs={{0,32},{32,0},{1,33},{33,1},{2,34},{34,2},{3,35},{35,3},{4,36},{36... | collective-permute-start | bytes 786440 | tf_op jit(solution)/shard_map/ppermute | solution.py:27
  105.0 17.4 %all-to-all-start.6 = ((f32[16,16,128]{2,1,0:T(8,128)}), f32[16,16,128]{2,1,0:T(8,128)S(1)}, u32[]{:S(2)}, u32[]{:S(2)}) async-start(f32[16,16,128]{2,1,0:T(8,128)} %get-tuple-element.33), calls=%async_computation.6 | async-start | bytes 262144 | tf_op jit(solution)/shard_map/all_to_all | solution.py:23

commit v6 on v5

--- a/solution.py
+++ b/solution.py
@@ -81,29 +81,8 @@
     return jnp.transpose(jnp.concatenate([part[:, :LINE], part[:, LINE:]], axis=0))
 
 
-def gram_of(packed):
-    both = lax.dot_general(packed, packed, (((0,), (0,)), ((), ())), precision=HIGH, preferred_element_type=F32)
-    return both[:64, :64] + both[64:, 64:]
-
-
-def shrink(gram):
-    blocks = gram[:32, :32], gram[32:, :32], gram[32:, 32:]
-    rows = [jnp.concatenate([block[8 * j : 8 * j + 8] for j in range(4)], axis=1) for block in blocks]
-    return jnp.concatenate(rows, axis=0)
-
-
-def grow(packed):
-    blocks = [
-        jnp.concatenate([packed[8 * i : 8 * i + 8, 32 * j : 32 * j + 32] for j in range(4)], axis=0) for i in range(3)
-    ]
-    lower = jnp.concatenate(
-        [
-            jnp.concatenate([blocks[0], jnp.zeros((32, 32), F32)], axis=1),
-            jnp.concatenate([blocks[1], blocks[2]], axis=1),
-        ],
-        axis=0,
-    )
-    return jnp.where(lax.broadcasted_iota(jnp.int32, (64, 64), 1) < 32, lower, jnp.transpose(lower))
+def gram_of(turned):
+    return lax.dot_general(turned, turned, (((1,), (1,)), ((), ())), precision=HIGH, preferred_element_type=F32)
 
 
 def inverse_cholesky(gram):
@@ -138,17 +117,6 @@
     return out[:, n:]
 
 
-def rider_of(dinv):
-    lane = lax.broadcasted_iota(jnp.int32, (8, 128), 1)
-    return jnp.where(lane % 64 < 32, dinv[:8], dinv[8:])
-
-
-def dinv_of(rider):
-    low = lax.broadcasted_iota(jnp.int32, (8, 128), 1) % 64 < 32
-    top = jnp.where(low, rider, pltpu.roll(rider, 32, 1))
-    return jnp.concatenate([top, jnp.where(low, pltpu.roll(rider, 96, 1), rider)], axis=0)
-
-
 def near_kernel(points_ref, out_ref):
     points = points_ref[...]
     for i in range(NN):
@@ -203,7 +171,7 @@
 
 def first_kernel(*refs):
     own_refs, other_refs = refs[:2], refs[2:4]
-    in_ref, part_ref, dinv_ref, deg_ref, dinvs_ref = refs[4:]
+    in_ref, part_ref, dinv_ref, rider_ref, deg_ref = refs[4:]
     head = in_ref[0, :8]
     for i in range(1, NF):
         head = head + in_ref[i, :8]
@@ -213,39 +181,42 @@
     lines = []
     for h in range(2):
         line = jnp.sum(jnp.where(sub == 2 * h + mine // 8, head, 0.0), axis=0, keepdims=True)
-        lines.append(pltpu.roll(jnp.broadcast_to(line, (8, 128)), (128 + HALF * h - HALF * (mine % 8)) % 128, 1))
+        line = pltpu.roll(jnp.broadcast_to(line, (8, 128)), (128 - HALF * (mine % 8)) % 128, 1)
+        line = jnp.where(lane < HALF, line, 0.0)
+        for shift in (16, 32, 64):
+            line = line + pltpu.roll(line, shift, 1)
+        lines.append(line)
     deg_ref[...] = jnp.where(lane < HALF, lines[0], lines[1])[0, :OWN]
-    turned = jnp.transpose(lax.rsqrt(head))
-    columns = [
-        jnp.broadcast_to(jnp.concatenate([turned[:, 2 * h + i : 2 * h + i + 1] for i in range(2)], axis=0), (LINE, 128))
-        for h in range(2)
-    ]
-    dinv = jnp.where(lax.broadcasted_iota(jnp.int32, (LINE, 128), 1) < 64, columns[0], columns[1])
-    dinvs_ref[...] = dinv
-    dinv_ref[...] = dinvs_ref[pl.ds(pl.multiple_of(mine * HALF, HALF), HALF)]
+    rider = lax.rsqrt(jnp.where(sub == 0, lines[0], lines[1]))
+    rider_ref[...] = rider
+    turned = jnp.transpose(rider)[:HALF]
+    first, last = (jnp.broadcast_to(turned[:, h : h + 1], (HALF, 128)) for h in range(2))
+    dinv_ref[...] = jnp.where(lax.broadcasted_iota(jnp.int32, (HALF, 128), 1) < 64, first, last)
+    inverse = lax.rsqrt(head)
+    inverse = jnp.concatenate([inverse[i : i + 1] for i in range(4)], axis=1)
     packed = jnp.concatenate([in_ref[i, 8:] for i in range(NF)], axis=0)
-    scaled = jnp.concatenate(split(turn_out(packed * dinv)), axis=0)
+    scaled = jnp.concatenate(split(turn_out(packed) * inverse), axis=0)
     for side, weights in enumerate((own_refs, other_refs)):
         part = turn_in(product(scaled, weights, 1))
         for i in range(NN):
             part_ref[i, HALF * side : HALF * side + HALF] = part[HALF * i : HALF * i + HALF]
 
 
-def half_kernel(in_ref, dinv_ref, out_ref):
+def half_kernel(in_ref, dinv_ref, rider_ref, out_ref):
     out_ref[: 2 * HALF] = total(in_ref)
-    out_ref[2 * HALF :] = dinv_ref[...]
+    out_ref[2 * HALF : 3 * HALF] = dinv_ref[...]
+    out_ref[3 * HALF :] = rider_ref[...]
 
 
 def update_kernel(in_ref, out_ref):
     core = lax.axis_index("core")
     mine, other = in_ref[core], in_ref[1 - core]
-    own_dinv, other_dinv = mine[2 * HALF :], other[2 * HALF :]
+    sub = lax.broadcasted_iota(jnp.int32, (8, 128), 0)
     payload = jnp.concatenate(
         [
-            (mine[:HALF] + other[HALF : 2 * HALF]) * own_dinv,
-            (mine[HALF : 2 * HALF] + other[:HALF]) * other_dinv,
-            rider_of(own_dinv),
-            rider_of(other_dinv),
+            (mine[:HALF] + other[HALF : 2 * HALF]) * mine[2 * HALF : 3 * HALF],
+            (mine[HALF : 2 * HALF] + other[:HALF]) * other[2 * HALF : 3 * HALF],
+            jnp.where(sub < 2, mine[3 * HALF :], pltpu.roll(other[3 * HALF :], 2, 0)),
         ],
         axis=0,
     )
@@ -256,23 +227,27 @@
 def second_kernel(*refs):
     sides = refs[:2], refs[2:4]
     in_ref, out_ref, gram_ref = refs[4:]
-    grams, parts = [], []
+    lane = lax.broadcasted_iota(jnp.int32, (8, 128), 1)
+    riders = []
+    for v in range(2):
+        rider = in_ref[8 * v, 2 * HALF :]
+        for i in range(1, 8):
+            rider = jnp.where(lane // HALF == i, in_ref[8 * v + i, 2 * HALF :], rider)
+        riders.append(rider)
+    gram, part = 0.0, 0.0
     for side, weights in enumerate(sides):
-        updates, scaled = [], []
-        for i in range(NN):
-            update = in_ref[i, HALF * side : HALF * side + HALF]
-            rider = in_ref[i, 2 * HALF + 8 * side : 2 * HALF + 8 * side + 8]
-            updates.append(update)
-            scaled.append(update * dinv_of(rider))
-        scaled = jnp.concatenate(split(turn_out(jnp.concatenate(scaled, axis=0))), axis=0)
-        parts.append(product(scaled, weights, 0))
-        grams.append(gram_of(jnp.concatenate(updates, axis=0)))
-    gram_ref[...] = shrink(grams[0] + grams[1])
-    gram = gram_ref[pl.ds(pl.multiple_of(lax.axis_index("core") * 8, 8), 16)]
-    part = turn_in(parts[0] + parts[1])
+        updates = jnp.concatenate([in_ref[i, HALF * side : HALF * side + HALF] for i in range(NN)], axis=0)
+        updates = turn_out(updates)
+        dinv = [rider[2 * side + h : 2 * side + h + 1] for h in range(2) for rider in riders]
+        scaled = jnp.concatenate(split(updates * jnp.concatenate(dinv, axis=1)), axis=0)
+        part = part + product(scaled, weights, 0)
+        gram = gram + gram_of(updates)
+    gram_ref[...] = fold(gram)
+    half = gram_ref[pl.ds(pl.multiple_of(lax.axis_index("core") * 16, 16), 16)]
+    part = turn_in(part)
     for i in range(NF):
         out_ref[i, :HALF] = part[HALF * i : HALF * i + HALF]
-        out_ref[i, HALF:] = gram
+        out_ref[i, HALF:] = half
 
 
 def collect_kernel(in_ref, dinv_ref, out_ref, gram_ref):
@@ -283,23 +258,22 @@
         out_ref[i] = update
 
 
-def factor_kernel(gram_ref, inverse_ref):
-    gram = jnp.concatenate([gram_ref[0], gram_ref[1, 8:]], axis=0)
-    turned = jnp.transpose(inverse_cholesky(grow(gram)))
+def factor_kernel(gram_ref, inverse_ref, both_ref):
+    inverse = inverse_cholesky(unfold(jnp.concatenate([gram_ref[0], gram_ref[1]], axis=0)))
+    inverse_ref[...] = inverse
+    turned = jnp.transpose(inverse)
     none = jnp.zeros_like(turned)
-    inverse_ref[:64] = jnp.concatenate([turned, none], axis=1)
-    inverse_ref[64:] = jnp.concatenate([none, turned], axis=1)
-
-
-def normalize_kernel(in_ref, inverse_ref, update_ref, out_ref, updates_ref):
-    update = jnp.concatenate([in_ref[i] for i in range(NF)], axis=0)
-    update = jnp.dot(update, inverse_ref[...], precision=HIGH, preferred_element_type=F32)
-    updates_ref[...] = update
-    mine = lax.axis_index(FAR)
-    update_ref[...] = updates_ref[pl.ds(pl.multiple_of(mine * HALF, HALF), HALF)]
-    gram = shrink(gram_of(update))
+    both_ref[:64] = jnp.concatenate([turned, none], axis=1)
+    both_ref[64:] = jnp.concatenate([none, turned], axis=1)
+
+
+def normalize_kernel(in_ref, inverse_ref, both_ref, update_ref, out_ref):
+    turned = turn_out(jnp.concatenate([in_ref[i] for i in range(NF)], axis=0))
+    gram = fold(gram_of(jnp.dot(inverse_ref[...], turned, precision=HIGH, preferred_element_type=F32)))
     for i in range(NN):
         out_ref[i] = gram
+    mine = in_ref[lax.axis_index(FAR)]
+    update_ref[...] = jnp.dot(mine, both_ref[...], precision=HIGH, preferred_element_type=F32)
 
 
 def relay_kernel(in_ref, out_ref):
@@ -307,7 +281,7 @@
 
 
 def final_kernel(in_ref, update_ref, out_ref):
-    inverse = inverse_cholesky(grow(total(in_ref)))
+    inverse = inverse_cholesky(unfold(total(in_ref)))
     out_ref[...] = lax.dot_general(
         unfold(update_ref[...]), inverse, (((1,), (1,)), ((), ())), precision=HIGH, preferred_element_type=F32
     )
@@ -342,38 +316,32 @@
         basis,
         name="weights",
     )
-    part, dinv, degree = call(
+    part, dinv, rider, degree = call(
         first_kernel,
-        [shape(NN, 2 * HALF, 128), shape(HALF, 128), shape(own)],
+        [shape(NN, 2 * HALF, 128), shape(HALF, 128), shape(8, 128), shape(own)],
         *weights,
         exchange(sums, FAR),
-        scratch=[pltpu.VMEM((LINE, 128), F32)],
         name="first_product",
     )
-    (part,) = call(half_kernel, [shape(3 * HALF, 128)], exchange(part, NEAR), dinv, name="half_update")
-    (update,) = call(update_kernel, [shape(NN, 2 * HALF + 16, 128)], lax.all_gather(part, "core"), name="first_update")
+    (part,) = call(half_kernel, [shape(3 * HALF + 8, 128)], exchange(part, NEAR), dinv, rider, name="half_update")
+    (update,) = call(update_kernel, [shape(NN, 2 * HALF + 8, 128)], lax.all_gather(part, "core"), name="first_update")
     (part,) = call(
         second_kernel,
-        [shape(NF, HALF + 16, 128)],
+        [shape(NF, 2 * HALF, 128)],
         *weights,
         exchange(update, NEAR),
-        scratch=[pltpu.VMEM((24, 128), F32)],
+        scratch=[pltpu.VMEM((32, 128), F32)],
         name="second_product",
     )
     update, gram = call(
         collect_kernel, [shape(NF, HALF, 128), shape(16, 128)], exchange(part, FAR), dinv, name="collect"
     )
     everyone = exchange(update, FAR)
-    (inverse,) = call(factor_kernel, [shape(128, 128)], lax.all_gather(gram, "core"), name="factor")
+    inverses = call(factor_kernel, [shape(64, 64), shape(128, 128)], lax.all_gather(gram, "core"), name="factor")
     update, gram = call(
-        normalize_kernel,
-        [shape(HALF, 128), shape(NN, 24, 128)],
-        everyone,
-        inverse,
-        scratch=[pltpu.VMEM((LINE, 128), F32)],
-        name="normalize",
-    )
-    (gram,) = call(relay_kernel, [shape(24, 128)], exchange(gram, NEAR), name="relay")
+        normalize_kernel, [shape(HALF, 128), shape(NN, 32, 128)], everyone, *inverses, name="normalize"
+    )
+    (gram,) = call(relay_kernel, [shape(32, 128)], exchange(gram, NEAR), name="relay")
     (out,) = call(final_kernel, [shape(own, 64)], lax.all_gather(gram, "core"), update, name="orthonormalize")
     return (out, degree)
 

time: 143 us -> 141 us (0.986)
  blocking collectives: 93.3 us -> 91.3 us
where the time goes in v6:
time: 141 us; the launch traced here: 140 us
  blocking collectives  91.3 us (65%)
  starting transfers between devices  23.8 us (17%)
  waiting for transfers between devices  13.7 us (10%)
  Pallas kernels  9.6 us (7%)
    all_to_all x6, blocking collectives, exchange(): return lax.all_to_all(chunks, axes, 0, 0, tiled=True)  76.1 us
    all_to_all x2, starting transfers between devices, exchange(): return lax.all_to_all(chunks, axes, 0, 0, tiled=True)  19.8 us
    all_to_all x2, waiting for transfers between devices, exchange(): return lax.all_to_all(chunks, axes, 0, 0, tiled=True)  12.7 us
    pallas_call x14, Pallas kernels, call(): pl.pallas_call(body, out_shape=outs, in_specs=specs or [VMEM] * len(args)...  9.6 us
    all_gather x2, blocking collectives, per_device(): lax.all_gather(gram, 'core')  9.01 us
    all_gather x1, blocking collectives, per_device(): lax.all_gather(part, 'core')  6.24 us
    ppermute x1, starting transfers between devices, swap(): return lax.ppermute(value, 'core', [(0, 1), (1, 0)])  4.02 us
  transfers between devices with their start and end apart: 3, of which 3 were waited for; matrix products, arithmetic and copies ran while one was open for 0% of the time, Pallas kernels for 2%

profile of v6, /device:TPU:1, one launch (start us, length us, event | category | flops | bytes accessed | tf_op | source)
XLA Modules:
  0.0 139.9 jit_solution(9887764970943375828)
XLA Ops:
  0.6 0.0 copy-start
  0.6 0.7 copy-done
  1.4 0.0 copy-start.1
  1.4 14.4 %all_to_all.40.near_ref.after_ref = bf16[16,32,256]{2,1,0:T(8,128)(2,1)S(1)} all-to-all(bf16[16,32,256]{2,1,0:T(8,128)(2,1)S(1)} %near_copies.1), channel_id=1, replica_groups=mesh['x'=4,'yh'=2,'core'=2,'ym'=2,'yl'=2,'zh'=4,'zl'=2] {'x','yl','zl'}, dimensions={0} | all-to-all | bytes 524288 | tf_op jit(solution)/shard_map/all_to_all | solution.py:23
  15.8 0.0 copy-done.1
  15.8 0.7 far_copies.1
  16.5 13.8 %all-to-all-start.1 = ((bf16[16,32,256]{2,1,0:T(8,128)(2,1)}), bf16[16,32,256]{2,1,0:T(8,128)(2,1)S(1)}, u32[]{:S(2)}, u32[]{:S(2)}) async-start(bf16[16,32,256]{2,1,0:T(8,128)(2,1)} %get-tuple-element.27), calls=%async_computation.1 | async-start | bytes 524288 | tf_op jit(solution)/shard_map/all_to_all | solution.py:23
  30.3 4.0 %collective-permute-start = (bf16[16,32,256]{2,1,0:T(8,128)(2,1)S(1)}, bf16[16,32,256]{2,1,0:T(8,128)(2,1)S(1)}, u32[]{:S(2)}, u32[]{:S(2)}) collective-permute-start(bf16[16,32,256]{2,1,0:T(8,128)(2,1)S(1)} %all_to_all.40.near_ref.after_ref), channel_id=1, source_target_pairs={{0,32},{32,0},{1,33},{33,1},{2,34},{34,2},{3,35},{35,3},{4,36},{36... | collective-permute-start | bytes 786440 | tf_op jit(solution)/shard_map/ppermute | solution.py:27
  34.3 0.1 own_line.1
  34.4 1.0 collective-permute-done.near_ref
  35.4 0.1 other_line.1
  35.6 6.6 %all-to-all-done.1.far_ref = bf16[16,32,256]{2,1,0:T(8,128)(2,1)S(1)} async-done(((bf16[16,32,256]{2,1,0:T(8,128)(2,1)}), bf16[16,32,256]{2,1,0:T(8,128)(2,1)S(1)}, u32[]{:S(2)}, u32[]{:S(2)}) %all-to-all-start.1) | async-done | bytes 262176 | tf_op jit(solution)/shard_map/all_to_all | solution.py:23
  42.2 0.8 weights.1
  43.0 16.5 %all_to_all.41.refs_4_ = f32[16,24,128]{2,1,0:T(8,128)S(1)} all-to-all(f32[16,24,128]{2,1,0:T(8,128)S(1)} %get-tuple-element.33), channel_id=1, replica_groups=mesh['x'=4,'yh'=2,'core'=2,'ym'=2,'yl'=2,'zh'=4,'zl'=2] {'yh','ym','zh'}, dimensions={0} | all-to-all | bytes 393216 | tf_op jit(solution)/shard_map/all_to_all | solution.py:23
  59.6 0.9 first_product.1
  60.5 10.2 %all_to_all.42.in_ref = f32[16,32,128]{2,1,0:T(8,128)S(1)} all-to-all(f32[16,32,128]{2,1,0:T(8,128)S(1)} %get-tuple-element.34), channel_id=1, replica_groups=mesh['x'=4,'yh'=2,'core'=2,'ym'=2,'yl'=2,'zh'=4,'zl'=2] {'x','yl','zl'}, dimensions={0} | all-to-all | bytes 524288 | tf_op jit(solution)/shard_map/all_to_all | solution.py:23
  70.8 6.2 %all-gather = f32[112,128]{1,0:T(8,128)S(1)} all-gather(f32[56,128]{1,0:T(8,128)S(1)} %half_update.1), channel_id=2, replica_groups=mesh['x'=4,'yh'=2,'core'=2,'ym'=2,'yl'=2,'zh'=4,'zl'=2] {'core'}, dimensions={0}, use_global_device_ids=true | all-gather | bytes 86016 | tf_op jit(solution)/shard_map/all_gather | solution.py:327
  77.0 9.9 %all_to_all.43.refs_4_ = f32[16,40,128]{2,1,0:T(8,128)S(1)} all-to-all(f32[16,40,128]{2,1,0:T(8,128)S(1)} %first_update.1), channel_id=1, replica_groups=mesh['x'=4,'yh'=2,'core'=2,'ym'=2,'yl'=2,'zh'=4,'zl'=2] {'x','yl','zl'}, dimensions={0} | all-to-all | bytes 655360 | tf_op jit(solution)/shard_map/all_to_all | solution.py:23
  87.0 0.9 second_product.1
  87.9 15.3 %all_to_all.44.in_ref = f32[16,32,128]{2,1,0:T(8,128)S(1)} all-to-all(f32[16,32,128]{2,1,0:T(8,128)S(1)} %second_product.1), channel_id=1, replica_groups=mesh['x'=4,'yh'=2,'core'=2,'ym'=2,'yl'=2,'zh'=4,'zl'=2] {'yh','ym','zh'}, dimensions={0} | all-to-all | bytes 524288 | tf_op jit(solution)/shard_map/all_to_all | solution.py:23
  103.1 0.7 collect.1
  103.8 6.0 %all-to-all-start.6 = ((f32[16,16,128]{2,1,0:T(8,128)}), f32[16,16,128]{2,1,0:T(8,128)S(1)}, u32[]{:S(2)}, u32[]{:S(2)}) async-start(f32[16,16,128]{2,1,0:T(8,128)} %get-tuple-element.37), calls=%async_computation.6 | async-start | bytes 262144 | tf_op jit(solution)/shard_map/all_to_all | solution.py:23
  109.9 3.3 %all-gather.1 = f32[32,128]{1,0:T(8,128)S(1)} all-gather(f32[16,128]{1,0:T(8,128)S(1)} %get-tuple-element.38), channel_id=3, replica_groups=mesh['x'=4,'yh'=2,'core'=2,'ym'=2,'yl'=2,'zh'=4,'zl'=2] {'core'}, dimensions={0}, use_global_device_ids=true | all-gather | bytes 24576 | tf_op jit(solution)/shard_map/all_gather | solution.py:340
  113.2 2.0 %factor.1 = (f32[64,64]{1,0:T(8,128)S(1)}, f32[128,128]{1,0:T(8,128)S(1)}) custom-call(f32[2,16,128]{2,1,0:T(8,128)S(1)} %bitcast.5), custom_call_target="tpu_custom_call" | custom-call | tf_op jit(solution)/shard_map/factor/pallas_call | solution.py:31
  115.2 6.1 %all-to-all-done.6.in_ref = f32[16,16,128]{2,1,0:T(8,128)S(1)} async-done(((f32[16,16,128]{2,1,0:T(8,128)}), f32[16,16,128]{2,1,0:T(8,128)S(1)}, u32[]{:S(2)}, u32[]{:S(2)}) %all-to-all-start.6) | async-done | bytes 131104 | tf_op jit(solution)/shard_map/all_to_all | solution.py:23
  121.3 0.7 normalize.1
  122.0 9.7 %all_to_all.45.in_ref = f32[16,32,128]{2,1,0:T(8,128)S(1)} all-to-all(f32[16,32,128]{2,1,0:T(8,128)S(1)} %get-tuple-element.41), channel_id=1, replica_groups=mesh['x'=4,'yh'=2,'core'=2,'ym'=2,'yl'=2,'zh'=4,'zl'=2] {'x','yl','zl'}, dimensions={0} | all-to-all | bytes 524288 | tf_op jit(solution)/shard_map/all_to_all | solution.py:23
  131.7 5.7 %all-gather.2 = f32[64,128]{1,0:T(8,128)S(1)} all-gather(f32[32,128]{1,0:T(8,128)S(1)} %relay.1), channel_id=4, replica_groups=mesh['x'=4,'yh'=2,'core'=2,'ym'=2,'yl'=2,'zh'=4,'zl'=2] {'core'}, dimensions={0}, use_global_device_ids=true | all-gather | bytes 49152 | tf_op jit(solution)/shard_map/all_gather | solution.py:345
  137.3 2.6 %orthonormalize.1 = f32[32,64]{1,0:T(8,128)} custom-call(f32[2,32,128]{2,1,0:T(8,128)S(1)} %bitcast.4, f32[16,128]{1,0:T(8,128)S(1)} %get-tuple-element.42.update_ref), custom_call_target="tpu_custom_call" | custom-call | tf_op jit(solution)/shard_map/orthonormalize/pallas_call | solution.py:31
  (4 shorter events, 0.1 us)
Async XLA Ops:
  0.6 0.7 copy-start
  1.4 14.4 %copy-start.1 = (f32[32,64]{1,0:T(8,128)S(1)}, f32[32,64]{1,0:T(8,128)}, u32[]{:S(2)}) copy-start(f32[32,64]{1,0:T(8,128)} %basis_ref.1) | copy-start | bytes 24580
  16.5 25.7 %all-to-all-start.1 = ((bf16[16,32,256]{2,1,0:T(8,128)(2,1)}), bf16[16,32,256]{2,1,0:T(8,128)(2,1)S(1)}, u32[]{:S(2)}, u32[]{:S(2)}) async-start(bf16[16,32,256]{2,1,0:T(8,128)(2,1)} %get-tuple-element.27), calls=%async_computation.1 | async-start | bytes 524288 | tf_op jit(solution)/shard_map/all_to_all | solution.py:23
  30.3 5.2 %collective-permute-start = (bf16[16,32,256]{2,1,0:T(8,128)(2,1)S(1)}, bf16[16,32,256]{2,1,0:T(8,128)(2,1)S(1)}, u32[]{:S(2)}, u32[]{:S(2)}) collective-permute-start(bf16[16,32,256]{2,1,0:T(8,128)(2,1)S(1)} %all_to_all.40.near_ref.after_ref), channel_id=1, source_target_pairs={{0,32},{32,0},{1,33},{33,1},{2,34},{34,2},{3,35},{35,3},{4,36},{36... | collective-permute-start | bytes 786440 | tf_op jit(solution)/shard_map/ppermute | solution.py:27
  103.8 17.5 %all-to-all-start.6 = ((f32[16,16,128]{2,1,0:T(8,128)}), f32[16,16,128]{2,1,0:T(8,128)S(1)}, u32[]{:S(2)}, u32[]{:S(2)}) async-start(f32[16,16,128]{2,1,0:T(8,128)} %get-tuple-element.37), calls=%async_computation.6 | async-start | bytes 262144 | tf_op jit(solution)/shard_map/all_to_all | solution.py:23

commit v7 on v6

--- a/solution.py
+++ b/solution.py
@@ -267,17 +267,17 @@
     both_ref[64:] = jnp.concatenate([none, turned], axis=1)
 
 
-def normalize_kernel(in_ref, inverse_ref, both_ref, update_ref, out_ref):
+def normalize_kernel(in_ref, inverse_ref, both_ref, update_ref, gram_ref):
     turned = turn_out(jnp.concatenate([in_ref[i] for i in range(NF)], axis=0))
-    gram = fold(gram_of(jnp.dot(inverse_ref[...], turned, precision=HIGH, preferred_element_type=F32)))
+    gram_ref[...] = fold(gram_of(jnp.dot(inverse_ref[...], turned, precision=HIGH, preferred_element_type=F32)))
+    mine = in_ref[lax.axis_index(FAR)]
+    update_ref[...] = jnp.dot(mine, both_ref[...], precision=HIGH, preferred_element_type=F32)
+
+
+def spread_kernel(in_ref, out_ref):
+    gram = total(in_ref)
     for i in range(NN):
         out_ref[i] = gram
-    mine = in_ref[lax.axis_index(FAR)]
-    update_ref[...] = jnp.dot(mine, both_ref[...], precision=HIGH, preferred_element_type=F32)
-
-
-def relay_kernel(in_ref, out_ref):
-    out_ref[...] = total(in_ref)
 
 
 def final_kernel(in_ref, update_ref, out_ref):
@@ -338,11 +338,9 @@
     )
     everyone = exchange(update, FAR)
     inverses = call(factor_kernel, [shape(64, 64), shape(128, 128)], lax.all_gather(gram, "core"), name="factor")
-    update, gram = call(
-        normalize_kernel, [shape(HALF, 128), shape(NN, 32, 128)], everyone, *inverses, name="normalize"
-    )
-    (gram,) = call(relay_kernel, [shape(32, 128)], exchange(gram, NEAR), name="relay")
-    (out,) = call(final_kernel, [shape(own, 64)], lax.all_gather(gram, "core"), update, name="orthonormalize")
+    update, gram = call(normalize_kernel, [shape(HALF, 128), shape(32, 128)], everyone, *inverses, name="normalize")
+    (gram,) = call(spread_kernel, [shape(NN, 32, 128)], lax.all_gather(gram, "core"), name="spread")
+    (out,) = call(final_kernel, [shape(own, 64)], exchange(gram, NEAR), update, name="orthonormalize")
     return (out, degree)
 
 

time: 141 us -> 140 us (level)
  no operation moved by 1% of the time
where the time goes in v7:
time: 140 us; the launch traced here: 139 us
  blocking collectives  90.3 us (64%)
  starting transfers between devices  23.8 us (17%)
  waiting for transfers between devices  13.7 us (10%)
  Pallas kernels  9.54 us (7%)
    all_to_all x6, blocking collectives, exchange(): return lax.all_to_all(chunks, axes, 0, 0, tiled=True)  76.2 us
    all_to_all x2, starting transfers between devices, exchange(): return lax.all_to_all(chunks, axes, 0, 0, tiled=True)  19.8 us
    all_to_all x2, waiting for transfers between devices, exchange(): return lax.all_to_all(chunks, axes, 0, 0, tiled=True)  12.7 us
    pallas_call x14, Pallas kernels, call(): pl.pallas_call(body, out_shape=outs, in_specs=specs or [VMEM] * len(args)...  9.54 us
    all_gather x2, blocking collectives, per_device(): lax.all_gather(gram, 'core')  7.89 us
    all_gather x1, blocking collectives, per_device(): lax.all_gather(part, 'core')  6.24 us
    ppermute x1, starting transfers between devices, swap(): return lax.ppermute(value, 'core', [(0, 1), (1, 0)])  4.02 us
  transfers between devices with their start and end apart: 3, of which 3 were waited for; matrix products, arithmetic and copies ran while one was open for 0% of the time, Pallas kernels for 2%

profile of v7, /device:TPU:1, one launch (start us, length us, event | category | flops | bytes accessed | tf_op | source)
XLA Modules:
  0.0 138.8 jit_solution(1660667404096470079)
XLA Ops:
  0.6 0.0 copy-start
  0.6 0.7 copy-done
  1.4 0.0 copy-start.1
  1.4 14.4 %all_to_all.40.near_ref.after_ref = bf16[16,32,256]{2,1,0:T(8,128)(2,1)S(1)} all-to-all(bf16[16,32,256]{2,1,0:T(8,128)(2,1)S(1)} %near_copies.1), channel_id=1, replica_groups=mesh['x'=4,'yh'=2,'core'=2,'ym'=2,'yl'=2,'zh'=4,'zl'=2] {'x','yl','zl'}, dimensions={0} | all-to-all | bytes 524288 | tf_op jit(solution)/shard_map/all_to_all | solution.py:23
  15.8 0.0 copy-done.1
  15.8 0.7 far_copies.1
  16.5 13.8 %all-to-all-start.1 = ((bf16[16,32,256]{2,1,0:T(8,128)(2,1)}), bf16[16,32,256]{2,1,0:T(8,128)(2,1)S(1)}, u32[]{:S(2)}, u32[]{:S(2)}) async-start(bf16[16,32,256]{2,1,0:T(8,128)(2,1)} %get-tuple-element.27), calls=%async_computation.1 | async-start | bytes 524288 | tf_op jit(solution)/shard_map/all_to_all | solution.py:23
  30.3 4.0 %collective-permute-start = (bf16[16,32,256]{2,1,0:T(8,128)(2,1)S(1)}, bf16[16,32,256]{2,1,0:T(8,128)(2,1)S(1)}, u32[]{:S(2)}, u32[]{:S(2)}) collective-permute-start(bf16[16,32,256]{2,1,0:T(8,128)(2,1)S(1)} %all_to_all.40.near_ref.after_ref), channel_id=1, source_target_pairs={{0,32},{32,0},{1,33},{33,1},{2,34},{34,2},{3,35},{35,3},{4,36},{36... | collective-permute-start | bytes 786440 | tf_op jit(solution)/shard_map/ppermute | solution.py:27
  34.3 0.1 own_line.1
  34.4 1.0 collective-permute-done.near_ref
  35.4 0.1 other_line.1
  35.6 6.6 %all-to-all-done.1.far_ref = bf16[16,32,256]{2,1,0:T(8,128)(2,1)S(1)} async-done(((bf16[16,32,256]{2,1,0:T(8,128)(2,1)}), bf16[16,32,256]{2,1,0:T(8,128)(2,1)S(1)}, u32[]{:S(2)}, u32[]{:S(2)}) %all-to-all-start.1) | async-done | bytes 262176 | tf_op jit(solution)/shard_map/all_to_all | solution.py:23
  42.2 0.8 weights.1
  43.0 16.5 %all_to_all.41.refs_4_ = f32[16,24,128]{2,1,0:T(8,128)S(1)} all-to-all(f32[16,24,128]{2,1,0:T(8,128)S(1)} %get-tuple-element.33), channel_id=1, replica_groups=mesh['x'=4,'yh'=2,'core'=2,'ym'=2,'yl'=2,'zh'=4,'zl'=2] {'yh','ym','zh'}, dimensions={0} | all-to-all | bytes 393216 | tf_op jit(solution)/shard_map/all_to_all | solution.py:23
  59.6 0.9 first_product.1
  60.5 10.2 %all_to_all.42.in_ref = f32[16,32,128]{2,1,0:T(8,128)S(1)} all-to-all(f32[16,32,128]{2,1,0:T(8,128)S(1)} %get-tuple-element.34), channel_id=1, replica_groups=mesh['x'=4,'yh'=2,'core'=2,'ym'=2,'yl'=2,'zh'=4,'zl'=2] {'x','yl','zl'}, dimensions={0} | all-to-all | bytes 524288 | tf_op jit(solution)/shard_map/all_to_all | solution.py:23
  70.8 6.2 %all-gather = f32[112,128]{1,0:T(8,128)S(1)} all-gather(f32[56,128]{1,0:T(8,128)S(1)} %half_update.1), channel_id=2, replica_groups=mesh['x'=4,'yh'=2,'core'=2,'ym'=2,'yl'=2,'zh'=4,'zl'=2] {'core'}, dimensions={0}, use_global_device_ids=true | all-gather | bytes 86016 | tf_op jit(solution)/shard_map/all_gather | solution.py:327
  77.0 9.9 %all_to_all.43.refs_4_ = f32[16,40,128]{2,1,0:T(8,128)S(1)} all-to-all(f32[16,40,128]{2,1,0:T(8,128)S(1)} %first_update.1), channel_id=1, replica_groups=mesh['x'=4,'yh'=2,'core'=2,'ym'=2,'yl'=2,'zh'=4,'zl'=2] {'x','yl','zl'}, dimensions={0} | all-to-all | bytes 655360 | tf_op jit(solution)/shard_map/all_to_all | solution.py:23
  87.0 0.9 second_product.1
  87.9 15.3 %all_to_all.44.in_ref = f32[16,32,128]{2,1,0:T(8,128)S(1)} all-to-all(f32[16,32,128]{2,1,0:T(8,128)S(1)} %second_product.1), channel_id=1, replica_groups=mesh['x'=4,'yh'=2,'core'=2,'ym'=2,'yl'=2,'zh'=4,'zl'=2] {'yh','ym','zh'}, dimensions={0} | all-to-all | bytes 524288 | tf_op jit(solution)/shard_map/all_to_all | solution.py:23
  103.1 0.7 collect.1
  103.8 6.0 %all-to-all-start.6 = ((f32[16,16,128]{2,1,0:T(8,128)}), f32[16,16,128]{2,1,0:T(8,128)S(1)}, u32[]{:S(2)}, u32[]{:S(2)}) async-start(f32[16,16,128]{2,1,0:T(8,128)} %get-tuple-element.37), calls=%async_computation.6 | async-start | bytes 262144 | tf_op jit(solution)/shard_map/all_to_all | solution.py:23
  109.9 3.3 %all-gather.1 = f32[32,128]{1,0:T(8,128)S(1)} all-gather(f32[16,128]{1,0:T(8,128)S(1)} %get-tuple-element.38), channel_id=3, replica_groups=mesh['x'=4,'yh'=2,'core'=2,'ym'=2,'yl'=2,'zh'=4,'zl'=2] {'core'}, dimensions={0}, use_global_device_ids=true | all-gather | bytes 24576 | tf_op jit(solution)/shard_map/all_gather | solution.py:340
  113.2 2.0 %factor.1 = (f32[64,64]{1,0:T(8,128)S(1)}, f32[128,128]{1,0:T(8,128)S(1)}) custom-call(f32[2,16,128]{2,1,0:T(8,128)S(1)} %bitcast.5), custom_call_target="tpu_custom_call" | custom-call | tf_op jit(solution)/shard_map/factor/pallas_call | solution.py:31
  115.2 6.1 %all-to-all-done.6.in_ref = f32[16,16,128]{2,1,0:T(8,128)S(1)} async-done(((f32[16,16,128]{2,1,0:T(8,128)}), f32[16,16,128]{2,1,0:T(8,128)S(1)}, u32[]{:S(2)}, u32[]{:S(2)}) %all-to-all-start.6) | async-done | bytes 131104 | tf_op jit(solution)/shard_map/all_to_all | solution.py:23
  121.3 0.6 normalize.1
  121.9 4.6 %all-gather.2 = f32[64,128]{1,0:T(8,128)S(1)} all-gather(f32[32,128]{1,0:T(8,128)S(1)} %get-tuple-element.41), channel_id=4, replica_groups=mesh['x'=4,'yh'=2,'core'=2,'ym'=2,'yl'=2,'zh'=4,'zl'=2] {'core'}, dimensions={0}, use_global_device_ids=true | all-gather | bytes 49152 | tf_op jit(solution)/shard_map/all_gather | solution.py:342
  126.5 9.8 %all_to_all.45.in_ref = f32[16,32,128]{2,1,0:T(8,128)S(1)} all-to-all(f32[16,32,128]{2,1,0:T(8,128)S(1)} %spread.1), channel_id=1, replica_groups=mesh['x'=4,'yh'=2,'core'=2,'ym'=2,'yl'=2,'zh'=4,'zl'=2] {'x','yl','zl'}, dimensions={0} | all-to-all | bytes 524288 | tf_op jit(solution)/shard_map/all_to_all | solution.py:23
  136.2 2.6 %orthonormalize.1 = f32[32,64]{1,0:T(8,128)} custom-call(f32[16,32,128]{2,1,0:T(8,128)S(1)} %all_to_all.45.in_ref, f32[16,128]{1,0:T(8,128)S(1)} %get-tuple-element.42.update_ref), custom_call_target="tpu_custom_call" | custom-call | tf_op jit(solution)/shard_map/orthonormalize/pallas_call | solution.py:31
  (4 shorter events, 0.1 us)
Async XLA Ops:
  0.6 0.7 copy-start
  1.4 14.4 %copy-start.1 = (f32[32,64]{1,0:T(8,128)S(1)}, f32[32,64]{1,0:T(8,128)}, u32[]{:S(2)}) copy-start(f32[32,64]{1,0:T(8,128)} %basis_ref.1) | copy-start | bytes 24580
  16.5 25.7 %all-to-all-start.1 = ((bf16[16,32,256]{2,1,0:T(8,128)(2,1)}), bf16[16,32,256]{2,1,0:T(8,128)(2,1)S(1)}, u32[]{:S(2)}, u32[]{:S(2)}) async-start(bf16[16,32,256]{2,1,0:T(8,128)(2,1)} %get-tuple-element.27), calls=%async_computation.1 | async-start | bytes 524288 | tf_op jit(solution)/shard_map/all_to_all | solution.py:23
  30.3 5.2 %collective-permute-start = (bf16[16,32,256]{2,1,0:T(8,128)(2,1)S(1)}, bf16[16,32,256]{2,1,0:T(8,128)(2,1)S(1)}, u32[]{:S(2)}, u32[]{:S(2)}) collective-permute-start(bf16[16,32,256]{2,1,0:T(8,128)(2,1)S(1)} %all_to_all.40.near_ref.after_ref), channel_id=1, source_target_pairs={{0,32},{32,0},{1,33},{33,1},{2,34},{34,2},{3,35},{35,3},{4,36},{36... | collective-permute-start | bytes 786440 | tf_op jit(solution)/shard_map/ppermute | solution.py:27
  103.8 17.5 %all-to-all-start.6 = ((f32[16,16,128]{2,1,0:T(8,128)}), f32[16,16,128]{2,1,0:T(8,128)S(1)}, u32[]{:S(2)}, u32[]{:S(2)}) async-start(f32[16,16,128]{2,1,0:T(8,128)} %get-tuple-element.37), calls=%async_computation.6 | async-start | bytes 262144 | tf_op jit(solution)/shard_map/all_to_all | solution.py:23

commit v8 on v7

--- a/solution.py
+++ b/solution.py
@@ -83,6 +83,18 @@
 
 def gram_of(turned):
     return lax.dot_general(turned, turned, (((1,), (1,)), ((), ())), precision=HIGH, preferred_element_type=F32)
+
+
+def shrink(gram):
+    strips = [gram[8 * j : 8 * j + 8, :32] for j in range(4)]
+    return jnp.concatenate([fold(gram[32:]), jnp.concatenate(strips, axis=1)], axis=0)
+
+
+def grow(packed):
+    lower = unfold(packed[:16])
+    block = jnp.concatenate([packed[16:, 32 * j : 32 * j + 32] for j in range(4)], axis=0)
+    upper = jnp.concatenate([block, jnp.transpose(lower)[:32]], axis=1)
+    return jnp.concatenate([upper, lower], axis=0)
 
 
 def inverse_cholesky(gram):
@@ -269,7 +281,7 @@
 
 def normalize_kernel(in_ref, inverse_ref, both_ref, update_ref, gram_ref):
     turned = turn_out(jnp.concatenate([in_ref[i] for i in range(NF)], axis=0))
-    gram_ref[...] = fold(gram_of(jnp.dot(inverse_ref[...], turned, precision=HIGH, preferred_element_type=F32)))
+    gram_ref[...] = shrink(gram_of(jnp.dot(inverse_ref[...], turned, precision=HIGH, preferred_element_type=F32)))
     mine = in_ref[lax.axis_index(FAR)]
     update_ref[...] = jnp.dot(mine, both_ref[...], precision=HIGH, preferred_element_type=F32)
 
@@ -281,7 +293,7 @@
 
 
 def final_kernel(in_ref, update_ref, out_ref):
-    inverse = inverse_cholesky(unfold(total(in_ref)))
+    inverse = inverse_cholesky(grow(total(in_ref)))
     out_ref[...] = lax.dot_general(
         unfold(update_ref[...]), inverse, (((1,), (1,)), ((), ())), precision=HIGH, preferred_element_type=F32
     )
@@ -338,8 +350,8 @@
     )
     everyone = exchange(update, FAR)
     inverses = call(factor_kernel, [shape(64, 64), shape(128, 128)], lax.all_gather(gram, "core"), name="factor")
-    update, gram = call(normalize_kernel, [shape(HALF, 128), shape(32, 128)], everyone, *inverses, name="normalize")
-    (gram,) = call(spread_kernel, [shape(NN, 32, 128)], lax.all_gather(gram, "core"), name="spread")
+    update, gram = call(normalize_kernel, [shape(HALF, 128), shape(24, 128)], everyone, *inverses, name="normalize")
+    (gram,) = call(spread_kernel, [shape(NN, 24, 128)], lax.all_gather(gram, "core"), name="spread")
     (out,) = call(final_kernel, [shape(own, 64)], exchange(gram, NEAR), update, name="orthonormalize")
     return (out, degree)
 

time: 140 us -> 139 us (level)
  no operation moved by 1% of the time
where the time goes in v8:
time: 139 us
  blocking collectives  89.9 us (65%)
  starting transfers between devices  23.8 us (17%)
  waiting for transfers between devices  13.7 us (10%)
  Pallas kernels  9.73 us (7%)
    all_to_all x6, blocking collectives, exchange(): return lax.all_to_all(chunks, axes, 0, 0, tiled=True)  75.8 us
    all_to_all x2, starting transfers between devices, exchange(): return lax.all_to_all(chunks, axes, 0, 0, tiled=True)  19.8 us
    all_to_all x2, waiting for transfers between devices, exchange(): return lax.all_to_all(chunks, axes, 0, 0, tiled=True)  12.7 us
    pallas_call x14, Pallas kernels, call(): pl.pallas_call(body, out_shape=outs, in_specs=specs or [VMEM] * len(args)...  9.73 us
    all_gather x2, blocking collectives, per_device(): lax.all_gather(gram, 'core')  7.89 us
    all_gather x1, blocking collectives, per_device(): lax.all_gather(part, 'core')  6.24 us
    ppermute x1, starting transfers between devices, swap(): return lax.ppermute(value, 'core', [(0, 1), (1, 0)])  4.02 us
  transfers between devices with their start and end apart: 3, of which 3 were waited for; matrix products, arithmetic and copies ran while one was open for 0% of the time, Pallas kernels for 2%

profile of v8, /device:TPU:1, one launch (start us, length us, event | category | flops | bytes accessed | tf_op | source)
XLA Modules:
  0.0 138.6 jit_solution(5040846767219017757)
XLA Ops:
  0.6 0.0 copy-start
  0.6 0.7 copy-done
  1.4 0.0 copy-start.1
  1.4 14.4 %all_to_all.40.near_ref.after_ref = bf16[16,32,256]{2,1,0:T(8,128)(2,1)S(1)} all-to-all(bf16[16,32,256]{2,1,0:T(8,128)(2,1)S(1)} %near_copies.1), channel_id=1, replica_groups=mesh['x'=4,'yh'=2,'core'=2,'ym'=2,'yl'=2,'zh'=4,'zl'=2] {'x','yl','zl'}, dimensions={0} | all-to-all | bytes 524288 | tf_op jit(solution)/shard_map/all_to_all | solution.py:23
  15.8 0.0 copy-done.1
  15.8 0.7 far_copies.1
  16.5 13.8 %all-to-all-start.1 = ((bf16[16,32,256]{2,1,0:T(8,128)(2,1)}), bf16[16,32,256]{2,1,0:T(8,128)(2,1)S(1)}, u32[]{:S(2)}, u32[]{:S(2)}) async-start(bf16[16,32,256]{2,1,0:T(8,128)(2,1)} %get-tuple-element.27), calls=%async_computation.1 | async-start | bytes 524288 | tf_op jit(solution)/shard_map/all_to_all | solution.py:23
  30.3 4.0 %collective-permute-start = (bf16[16,32,256]{2,1,0:T(8,128)(2,1)S(1)}, bf16[16,32,256]{2,1,0:T(8,128)(2,1)S(1)}, u32[]{:S(2)}, u32[]{:S(2)}) collective-permute-start(bf16[16,32,256]{2,1,0:T(8,128)(2,1)S(1)} %all_to_all.40.near_ref.after_ref), channel_id=1, source_target_pairs={{0,32},{32,0},{1,33},{33,1},{2,34},{34,2},{3,35},{35,3},{4,36},{36... | collective-permute-start | bytes 786440 | tf_op jit(solution)/shard_map/ppermute | solution.py:27
  34.3 0.1 own_line.1
  34.4 1.0 collective-permute-done.near_ref
  35.4 0.1 other_line.1
  35.6 6.6 %all-to-all-done.1.far_ref = bf16[16,32,256]{2,1,0:T(8,128)(2,1)S(1)} async-done(((bf16[16,32,256]{2,1,0:T(8,128)(2,1)}), bf16[16,32,256]{2,1,0:T(8,128)(2,1)S(1)}, u32[]{:S(2)}, u32[]{:S(2)}) %all-to-all-start.1) | async-done | bytes 262176 | tf_op jit(solution)/shard_map/all_to_all | solution.py:23
  42.2 0.8 weights.1
  43.0 16.5 %all_to_all.41.refs_4_ = f32[16,24,128]{2,1,0:T(8,128)S(1)} all-to-all(f32[16,24,128]{2,1,0:T(8,128)S(1)} %get-tuple-element.33), channel_id=1, replica_groups=mesh['x'=4,'yh'=2,'core'=2,'ym'=2,'yl'=2,'zh'=4,'zl'=2] {'yh','ym','zh'}, dimensions={0} | all-to-all | bytes 393216 | tf_op jit(solution)/shard_map/all_to_all | solution.py:23
  59.6 0.9 first_product.1
  60.5 10.2 %all_to_all.42.in_ref = f32[16,32,128]{2,1,0:T(8,128)S(1)} all-to-all(f32[16,32,128]{2,1,0:T(8,128)S(1)} %get-tuple-element.34), channel_id=1, replica_groups=mesh['x'=4,'yh'=2,'core'=2,'ym'=2,'yl'=2,'zh'=4,'zl'=2] {'x','yl','zl'}, dimensions={0} | all-to-all | bytes 524288 | tf_op jit(solution)/shard_map/all_to_all | solution.py:23
  70.8 6.2 %all-gather = f32[112,128]{1,0:T(8,128)S(1)} all-gather(f32[56,128]{1,0:T(8,128)S(1)} %half_update.1), channel_id=2, replica_groups=mesh['x'=4,'yh'=2,'core'=2,'ym'=2,'yl'=2,'zh'=4,'zl'=2] {'core'}, dimensions={0}, use_global_device_ids=true | all-gather | bytes 86016 | tf_op jit(solution)/shard_map/all_gather | solution.py:339
  77.0 9.9 %all_to_all.43.refs_4_ = f32[16,40,128]{2,1,0:T(8,128)S(1)} all-to-all(f32[16,40,128]{2,1,0:T(8,128)S(1)} %first_update.1), channel_id=1, replica_groups=mesh['x'=4,'yh'=2,'core'=2,'ym'=2,'yl'=2,'zh'=4,'zl'=2] {'x','yl','zl'}, dimensions={0} | all-to-all | bytes 655360 | tf_op jit(solution)/shard_map/all_to_all | solution.py:23
  87.0 0.9 second_product.1
  87.9 15.3 %all_to_all.44.in_ref = f32[16,32,128]{2,1,0:T(8,128)S(1)} all-to-all(f32[16,32,128]{2,1,0:T(8,128)S(1)} %second_product.1), channel_id=1, replica_groups=mesh['x'=4,'yh'=2,'core'=2,'ym'=2,'yl'=2,'zh'=4,'zl'=2] {'yh','ym','zh'}, dimensions={0} | all-to-all | bytes 524288 | tf_op jit(solution)/shard_map/all_to_all | solution.py:23
  103.1 0.7 collect.1
  103.8 6.0 %all-to-all-start.6 = ((f32[16,16,128]{2,1,0:T(8,128)}), f32[16,16,128]{2,1,0:T(8,128)S(1)}, u32[]{:S(2)}, u32[]{:S(2)}) async-start(f32[16,16,128]{2,1,0:T(8,128)} %get-tuple-element.37), calls=%async_computation.6 | async-start | bytes 262144 | tf_op jit(solution)/shard_map/all_to_all | solution.py:23
  109.9 3.3 %all-gather.1 = f32[32,128]{1,0:T(8,128)S(1)} all-gather(f32[16,128]{1,0:T(8,128)S(1)} %get-tuple-element.38), channel_id=3, replica_groups=mesh['x'=4,'yh'=2,'core'=2,'ym'=2,'yl'=2,'zh'=4,'zl'=2] {'core'}, dimensions={0}, use_global_device_ids=true | all-gather | bytes 24576 | tf_op jit(solution)/shard_map/all_gather | solution.py:352
  113.2 2.0 %factor.1 = (f32[64,64]{1,0:T(8,128)S(1)}, f32[128,128]{1,0:T(8,128)S(1)}) custom-call(f32[2,16,128]{2,1,0:T(8,128)S(1)} %bitcast.5), custom_call_target="tpu_custom_call" | custom-call | tf_op jit(solution)/shard_map/factor/pallas_call | solution.py:31
  115.2 6.1 %all-to-all-done.6.in_ref = f32[16,16,128]{2,1,0:T(8,128)S(1)} async-done(((f32[16,16,128]{2,1,0:T(8,128)}), f32[16,16,128]{2,1,0:T(8,128)S(1)}, u32[]{:S(2)}, u32[]{:S(2)}) %all-to-all-start.6) | async-done | bytes 131104 | tf_op jit(solution)/shard_map/all_to_all | solution.py:23
  121.3 0.6 normalize.1
  121.9 4.6 %all-gather.2 = f32[48,128]{1,0:T(8,128)S(1)} all-gather(f32[24,128]{1,0:T(8,128)S(1)} %get-tuple-element.41), channel_id=4, replica_groups=mesh['x'=4,'yh'=2,'core'=2,'ym'=2,'yl'=2,'zh'=4,'zl'=2] {'core'}, dimensions={0}, use_global_device_ids=true | all-gather | bytes 36864 | tf_op jit(solution)/shard_map/all_gather | solution.py:354
  126.5 9.4 %all_to_all.45.in_ref = f32[16,24,128]{2,1,0:T(8,128)S(1)} all-to-all(f32[16,24,128]{2,1,0:T(8,128)S(1)} %spread.1), channel_id=1, replica_groups=mesh['x'=4,'yh'=2,'core'=2,'ym'=2,'yl'=2,'zh'=4,'zl'=2] {'x','yl','zl'}, dimensions={0} | all-to-all | bytes 393216 | tf_op jit(solution)/shard_map/all_to_all | solution.py:23
  135.8 2.8 %orthonormalize.1 = f32[32,64]{1,0:T(8,128)} custom-call(f32[16,24,128]{2,1,0:T(8,128)S(1)} %all_to_all.45.in_ref, f32[16,128]{1,0:T(8,128)S(1)} %get-tuple-element.42.update_ref), custom_call_target="tpu_custom_call" | custom-call | tf_op jit(solution)/shard_map/orthonormalize/pallas_call | solution.py:31
  (4 shorter events, 0.1 us)
Async XLA Ops:
  0.6 0.7 copy-start
  1.4 14.4 %copy-start.1 = (f32[32,64]{1,0:T(8,128)S(1)}, f32[32,64]{1,0:T(8,128)}, u32[]{:S(2)}) copy-start(f32[32,64]{1,0:T(8,128)} %basis_ref.1) | copy-start | bytes 24580
  16.5 25.7 %all-to-all-start.1 = ((bf16[16,32,256]{2,1,0:T(8,128)(2,1)}), bf16[16,32,256]{2,1,0:T(8,128)(2,1)S(1)}, u32[]{:S(2)}, u32[]{:S(2)}) async-start(bf16[16,32,256]{2,1,0:T(8,128)(2,1)} %get-tuple-element.27), calls=%async_computation.1 | async-start | bytes 524288 | tf_op jit(solution)/shard_map/all_to_all | solution.py:23
  30.3 5.2 %collective-permute-start = (bf16[16,32,256]{2,1,0:T(8,128)(2,1)S(1)}, bf16[16,32,256]{2,1,0:T(8,128)(2,1)S(1)}, u32[]{:S(2)}, u32[]{:S(2)}) collective-permute-start(bf16[16,32,256]{2,1,0:T(8,128)(2,1)S(1)} %all_to_all.40.near_ref.after_ref), channel_id=1, source_target_pairs={{0,32},{32,0},{1,33},{33,1},{2,34},{34,2},{3,35},{35,3},{4,36},{36... | collective-permute-start | bytes 786440 | tf_op jit(solution)/shard_map/ppermute | solution.py:27
  103.8 17.5 %all-to-all-start.6 = ((f32[16,16,128]{2,1,0:T(8,128)}), f32[16,16,128]{2,1,0:T(8,128)S(1)}, u32[]{:S(2)}, u32[]{:S(2)}) async-start(f32[16,16,128]{2,1,0:T(8,128)} %get-tuple-element.37), calls=%async_computation.6 | async-start | bytes 262144 | tf_op jit(solution)/shard_map/all_to_all | solution.py:23
